TPU v7x, 32 devices: a whole 2x2x4 slice. The times are simulated.
32 devices in a mesh: section: 4 (over y, x), dp: 8 (over z, core).
Axes of the slice: x: 2, y: 2, z: 4, core: 2. Of those that a mesh axis runs over, the one named last changes fastest.
Arguments:
- image: bfloat16 [2, 2, 32, 7, 7, 2048], P(None, None, 'dp')
- section_weights: bfloat16 [4, 9456, 512], P('section')
- section_norms: float32 [4, 3, 2048], P('section'), as said below
- queue: bfloat16 [2, 512, 128], P(None, 'dp'), may hold values from -0.5 to 0.5
- pairing: int32 [2, 32], P(None, 'dp'), may hold values from 0 to 3, as said below
Outputs:
- loss: float32 [], replicated
- grad_input: float32 [2, 2, 32, 7, 7, 2048], P(None, None, 'dp', None, None, 'section')
- grad_weights: float32 [4, 9456, 512], P('section', None, 'dp')
- grad_norms: float32 [4, 3, 2048], P('section')
Inputs may be any that keep to these rules, and one draw needn't show every extreme that they name: `pairing`: each run of 4 entries of a row (the images of one index of dp) is a permutation of 0 to 3. `section_norms`: row 0 (gains) is positive.
All inputs are finite; a program needn't handle non-finite values.
Results may differ from a plain program's by a relative error of at most 0.025.
Values may be sent and summed in bfloat16 or wider, within the bound.
No kernel may reach another device: no remote copies, remote signals or barrier semaphores. Data moves between devices by JAX's collectives and lax.ppermute only.
A program may use at most 448 MiB of HBM per device.

v0:
```python
import jax
import jax.numpy as jnp
from jax import lax
from jax.sharding import PartitionSpec as P

D = 2048
BOTTLENECK_WIDTH = 512
PROJ = 128
PROTOS = 3000
SIDE = 7
IMAGE_CROPS = 2


NORM_EPS = 1e-05
UNIT_EPS = 1e-06
SINK_EPS = 0.05
TEMPER = 0.1
HIGH = lax.Precision.HIGHEST


def shifted(value, axis, steps):
    count = lax.axis_size(axis)
    first, last = (max(0, -steps), min(count, count - steps))
    return lax.ppermute(value, axis, [(source, source + steps) for source in range(first, last)])


def swish_slope(value):
    sigma = jax.nn.sigmoid(value)
    return sigma * (1.0 + value * (1.0 - sigma))


def picked_value(buffer, section_index):
    return lax.dynamic_index_in_dim(buffer, section_index, 0, keepdims=False)


def place(buffer, section_index, value, valid_mask):
    kept = jnp.where(valid_mask, value.astype(buffer.dtype), picked_value(buffer, section_index))
    return lax.dynamic_update_index_in_dim(buffer, kept, section_index, 0)


def balance_each(prototype_scores, queued_scores):
    mass = jnp.exp(jnp.concatenate([queued_scores, prototype_scores], axis=1) / SINK_EPS)
    for turn in range(3):
        column = lax.psum(jnp.sum(mass, axis=1), "dp")
        mass = mass / column[:, None, :]
        mass = mass / jnp.sum(mass, axis=2, keepdims=True)
    return mass[:, queued_scores.shape[1] :]


def body(image, section_weights, section_norms, queue, pairing):
    micro = image.shape[0]
    count_img = image.shape[2]
    input_rows = IMAGE_CROPS * count_img
    places = SIDE * SIDE
    cells = input_rows * places
    packed_rows = input_rows * D // BOTTLENECK_WIDTH
    ndp = lax.axis_size("dp")
    relay_section = lax.axis_index("section")
    packed = section_weights[0]
    norm_gains = section_norms[0]
    first = D * (D // BOTTLENECK_WIDTH)
    second = first + D * PROJ // BOTTLENECK_WIDTH
    third = second + PROTOS * PROJ // BOTTLENECK_WIDTH
    w_reduce = packed[:D]
    w_conv = packed[: 9 * BOTTLENECK_WIDTH].reshape(9, BOTTLENECK_WIDTH, BOTTLENECK_WIDTH)
    w_expand = packed[:D].reshape(BOTTLENECK_WIDTH, D)
    w_head = packed[:first].reshape(D, D)
    w_proj = packed[first:second].reshape(D, PROJ)
    protos = packed[second:third].reshape(PROTOS, PROJ)
    queued_scores = jnp.einsum("cqp,kp->cqk", queue, protos, preferred_element_type=jnp.float32)
    counted_rows = jnp.where(relay_section == 3, input_rows * ndp, cells * ndp).astype(jnp.float32)
    scale_all = 1.0 / (TEMPER * IMAGE_CROPS * count_img * ndp * micro)
    blank_scores = jnp.zeros((IMAGE_CROPS, count_img, PROTOS), jnp.float32)
    blank_message = jnp.zeros((cells, BOTTLENECK_WIDTH), jnp.bfloat16)
    blank_piece = jnp.zeros((cells, D), jnp.float32)
    zero_extra = jnp.zeros((D,), jnp.float32)

    def image_row_block(section_index):
        return picked_value(image, section_index).reshape(cells, D)

    def widen(value):
        return jnp.pad(value, ((0, cells - value.shape[0]), (0, D - value.shape[1])))

    def narrow_message(value):
        return jnp.pad(
            value.reshape(packed_rows, BOTTLENECK_WIDTH), ((0, cells - packed_rows), (0, 0))
        )

    def taps_of(flat):
        grid = jnp.pad(
            flat.reshape(input_rows, SIDE, SIDE, BOTTLENECK_WIDTH), ((0, 0), (1, 1), (1, 1), (0, 0))
        )
        return [
            grid[:, tap // 3 : tap // 3 + SIDE, tap % 3 : tap % 3 + SIDE].reshape(
                cells, BOTTLENECK_WIDTH
            )
            for tap in range(9)
        ]

    def front_reduce(incoming_message, section_index):
        return widen(
            jnp.dot(image_row_block(section_index), w_reduce, preferred_element_type=jnp.float32)
        )

    def front_conv(incoming_message, section_index):
        windows = taps_of(incoming_message)
        total = jnp.zeros((cells, BOTTLENECK_WIDTH), jnp.float32)
        for tap in range(9):
            total = total + jnp.dot(windows[tap], w_conv[tap], preferred_element_type=jnp.float32)
        return widen(total)

    def front_expand(incoming_message, section_index):
        return jnp.dot(incoming_message, w_expand, preferred_element_type=jnp.float32)

    def front_head(incoming_message, section_index):
        pooled = incoming_message[:packed_rows].reshape(input_rows, D)
        return widen(jnp.dot(pooled, w_head, preferred_element_type=jnp.float32))

    def narrow_backward(normalized_input, section_index):
        active_mask = jax.nn.silu(
            normalized_input[:, :BOTTLENECK_WIDTH] * norm_gains[0, :BOTTLENECK_WIDTH]
            + norm_gains[1, :BOTTLENECK_WIDTH]
        ).astype(jnp.bfloat16)
        return (active_mask, blank_scores)

    def expand_backward(normalized_input, section_index):
        summed_values = (
            normalized_input * norm_gains[0]
            + norm_gains[1]
            + image_row_block(section_index).astype(jnp.float32)
        )
        pooled = jnp.mean(jax.nn.silu(summed_values).reshape(input_rows, places, D), axis=1).astype(
            jnp.bfloat16
        )
        return (narrow_message(pooled), blank_scores)

    def head_backward(normalized_input, section_index):
        active_mask = jax.nn.silu(
            normalized_input[:input_rows] * norm_gains[0] + norm_gains[1]
        ).astype(jnp.bfloat16)
        embed = (
            jnp.dot(active_mask, w_proj, preferred_element_type=jnp.float32) + norm_gains[2, :PROJ]
        )
        unit = (embed * lax.rsqrt(jnp.sum(embed * embed, axis=1, keepdims=True) + UNIT_EPS)).astype(
            jnp.bfloat16
        )
        prototype_scores = jnp.einsum("rp,kp->rk", unit, protos, preferred_element_type=jnp.float32)
        return (blank_message, prototype_scores.reshape(IMAGE_CROPS, count_img, PROTOS))

    def forward_tick(tick, carry):
        message, saved_preactivation, keep_in, keep_stats, keep_scores, keep_codes = carry
        incoming_message = shifted(message, "section", 1)
        raw = tick - relay_section
        valid_mask = (raw >= 0) & (raw < micro)
        section_index = jnp.clip(raw, 0, micro - 1)
        preactivation = lax.switch(
            relay_section,
            [front_reduce, front_conv, front_expand, front_head],
            incoming_message,
            section_index,
        )
        partial_sums = jnp.stack(
            [jnp.sum(preactivation, axis=0), jnp.sum(preactivation * preactivation, axis=0)]
        )
        norm_statistics = lax.psum(partial_sums, "dp")
        batch_mean = norm_statistics[0] / counted_rows
        inverse_deviation = lax.rsqrt(
            norm_statistics[1] / counted_rows - batch_mean * batch_mean + NORM_EPS
        )
        normalized_input = (preactivation - batch_mean) * inverse_deviation
        message, prototype_scores = lax.switch(
            relay_section,
            [narrow_backward, narrow_backward, expand_backward, head_backward],
            normalized_input,
            section_index,
        )
        saved_preactivation = place(saved_preactivation, section_index, preactivation, valid_mask)
        keep_in = place(keep_in, section_index, incoming_message, valid_mask)
        keep_stats = place(
            keep_stats, section_index, jnp.stack([batch_mean, inverse_deviation]), valid_mask
        )
        keep_scores = place(keep_scores, section_index, prototype_scores, valid_mask)
        keep_codes = place(
            keep_codes, section_index, balance_each(prototype_scores, queued_scores), valid_mask
        )
        return (message, saved_preactivation, keep_in, keep_stats, keep_scores, keep_codes)

    start = (
        blank_message,
        jnp.zeros((micro, cells, D), jnp.float32),
        jnp.zeros((micro, cells, BOTTLENECK_WIDTH), jnp.bfloat16),
        jnp.zeros((micro, 2, D), jnp.float32),
        jnp.zeros((micro, IMAGE_CROPS, count_img, PROTOS), jnp.float32),
        jnp.zeros((micro, IMAGE_CROPS, count_img, PROTOS), jnp.float32),
    )
    final = lax.fori_loop(0, micro + 3, forward_tick, start)
    saved_preactivation, keep_in, keep_stats, keep_scores, keep_codes = (
        final[1],
        final[2],
        final[3],
        final[4],
        final[5],
    )

    def narrow_forward(
        incoming_message, normalized_input, section_index, valid_mask, gradient_list, summed_loss
    ):
        output_value = (
            normalized_input[:, :BOTTLENECK_WIDTH] * norm_gains[0, :BOTTLENECK_WIDTH]
            + norm_gains[1, :BOTTLENECK_WIDTH]
        )
        return (
            widen(incoming_message.astype(jnp.float32) * swish_slope(output_value)),
            zero_extra,
            gradient_list,
            summed_loss,
        )

    def expand_forward(
        incoming_message, normalized_input, section_index, valid_mask, gradient_list, summed_loss
    ):
        d_pooled = (
            incoming_message[:packed_rows].reshape(input_rows, 1, D).astype(jnp.float32) / places
        )
        summed_values = (
            normalized_input * norm_gains[0]
            + norm_gains[1]
            + image_row_block(section_index).astype(jnp.float32)
        )
        d_out = jnp.broadcast_to(d_pooled, (input_rows, places, D)).reshape(cells, D)
        return (d_out * swish_slope(summed_values), zero_extra, gradient_list, summed_loss)

    def head_forward(
        incoming_message, normalized_input, section_index, valid_mask, gradient_list, summed_loss
    ):
        output_value = normalized_input[:input_rows] * norm_gains[0] + norm_gains[1]
        active_mask = jax.nn.silu(output_value).astype(jnp.bfloat16)
        embed = (
            jnp.dot(active_mask, w_proj, preferred_element_type=jnp.float32) + norm_gains[2, :PROJ]
        )
        recip = lax.rsqrt(jnp.sum(embed * embed, axis=1, keepdims=True) + UNIT_EPS)
        unit = (embed * recip).astype(jnp.bfloat16)
        prototype_scores = picked_value(keep_scores, section_index).reshape(input_rows, PROTOS)
        assigned_codes = picked_value(keep_codes, section_index)
        onehot = (
            picked_value(pairing, section_index)[:, None]
            == jnp.arange(count_img, dtype=jnp.int32)[None, :]
        ).astype(jnp.float32)
        target = jnp.concatenate(
            [
                jnp.dot(onehot, assigned_codes[1], precision=HIGH),
                jnp.dot(onehot.T, assigned_codes[0], precision=HIGH),
            ]
        )
        logp = jax.nn.log_softmax(prototype_scores / TEMPER, axis=1)
        summed_loss = summed_loss + jnp.where(
            valid_mask, -jnp.sum(target * logp) * (TEMPER * scale_all), 0.0
        )
        d_scores = (
            (jnp.exp(logp) * jnp.sum(target, axis=1, keepdims=True) - target) * scale_all
        ).astype(jnp.bfloat16)
        d_unit = jnp.dot(d_scores, protos, preferred_element_type=jnp.float32)
        d_embed = (
            recip * d_unit - embed * recip**3 * jnp.sum(d_unit * embed, axis=1, keepdims=True)
        ).astype(jnp.bfloat16)
        g_protos = jnp.einsum("rk,rp->kp", d_scores, unit, preferred_element_type=jnp.float32)
        g_proj = jnp.einsum("rd,rp->dp", active_mask, d_embed, preferred_element_type=jnp.float32)
        gradient_list = gradient_list.at[first:second].add(
            jnp.where(valid_mask, g_proj.reshape(second - first, BOTTLENECK_WIDTH), 0.0)
        )
        gradient_list = gradient_list.at[second:third].add(
            jnp.where(valid_mask, g_protos.reshape(third - second, BOTTLENECK_WIDTH), 0.0)
        )
        extra_state = jnp.pad(jnp.sum(d_embed.astype(jnp.float32), axis=0), (0, D - PROJ))
        d_active = jnp.einsum("rp,dp->rd", d_embed, w_proj, preferred_element_type=jnp.float32)
        return (
            widen(d_active * swish_slope(output_value)),
            extra_state,
            gradient_list,
            summed_loss,
        )

    def end_reduce(
        preactivation_gradient, output_gradient, section_index, valid_mask, gradient_list
    ):
        d_low = preactivation_gradient[:, :BOTTLENECK_WIDTH].astype(jnp.bfloat16)
        g_reduce = jnp.einsum(
            "rd,rk->dk", image_row_block(section_index), d_low, preferred_element_type=jnp.float32
        )
        gradient_list = gradient_list.at[:D].add(jnp.where(valid_mask, g_reduce, 0.0))
        piece = jnp.einsum("rk,dk->rd", d_low, w_reduce, preferred_element_type=jnp.float32)
        return (blank_message, gradient_list, piece)

    def end_conv(preactivation_gradient, output_gradient, section_index, valid_mask, gradient_list):
        d_low = preactivation_gradient[:, :BOTTLENECK_WIDTH].astype(jnp.bfloat16)
        windows = taps_of(picked_value(keep_in, section_index))
        g_conv = jnp.stack(
            [
                jnp.einsum("rc,rk->ck", windows[tap], d_low, preferred_element_type=jnp.float32)
                for tap in range(9)
            ]
        )
        gradient_list = gradient_list.at[: 9 * BOTTLENECK_WIDTH].add(
            jnp.where(valid_mask, g_conv.reshape(9 * BOTTLENECK_WIDTH, BOTTLENECK_WIDTH), 0.0)
        )
        back = jnp.zeros((input_rows, SIDE + 2, SIDE + 2, BOTTLENECK_WIDTH), jnp.float32)
        for tap in range(9):
            part_back = jnp.einsum(
                "rk,ck->rc", d_low, w_conv[tap], preferred_element_type=jnp.float32
            ).reshape(input_rows, SIDE, SIDE, BOTTLENECK_WIDTH)
            back = back + jnp.pad(
                part_back, ((0, 0), (tap // 3, 2 - tap // 3), (tap % 3, 2 - tap % 3), (0, 0))
            )
        message = (
            back[:, 1 : SIDE + 1, 1 : SIDE + 1]
            .reshape(cells, BOTTLENECK_WIDTH)
            .astype(jnp.bfloat16)
        )
        return (message, gradient_list, blank_piece)

    def end_expand(
        preactivation_gradient, output_gradient, section_index, valid_mask, gradient_list
    ):
        d_low = preactivation_gradient.astype(jnp.bfloat16)
        g_expand = jnp.einsum(
            "rk,rd->kd",
            picked_value(keep_in, section_index),
            d_low,
            preferred_element_type=jnp.float32,
        )
        gradient_list = gradient_list.at[:D].add(
            jnp.where(valid_mask, g_expand.reshape(D, BOTTLENECK_WIDTH), 0.0)
        )
        message = jnp.einsum(
            "rd,kd->rk", d_low, w_expand, preferred_element_type=jnp.float32
        ).astype(jnp.bfloat16)
        return (message, gradient_list, output_gradient)

    def end_head(preactivation_gradient, output_gradient, section_index, valid_mask, gradient_list):
        d_low = preactivation_gradient[:input_rows].astype(jnp.bfloat16)
        pooled = picked_value(keep_in, section_index)[:packed_rows].reshape(input_rows, D)
        g_head = jnp.einsum("rd,re->de", pooled, d_low, preferred_element_type=jnp.float32)
        gradient_list = gradient_list.at[:first].add(
            jnp.where(valid_mask, g_head.reshape(first, BOTTLENECK_WIDTH), 0.0)
        )
        d_pooled = jnp.einsum(
            "re,de->rd", d_low, w_head, preferred_element_type=jnp.float32
        ).astype(jnp.bfloat16)
        return (narrow_message(d_pooled), gradient_list, blank_piece)

    def backward_tick(tick, carry):
        message, gradient_list, grad_in, norm_sum, summed_loss = carry
        incoming_message = shifted(message, "section", -1)
        raw = tick - (3 - relay_section)
        valid_mask = (raw >= 0) & (raw < micro)
        section_index = jnp.clip(raw, 0, micro - 1)
        norm_statistics = picked_value(keep_stats, section_index)
        normalized_input = (
            picked_value(saved_preactivation, section_index) - norm_statistics[0]
        ) * norm_statistics[1]
        local = gradient_list
        output_gradient, extra_state, local, summed_loss = lax.switch(
            relay_section,
            [narrow_forward, narrow_forward, expand_forward, head_forward],
            incoming_message,
            normalized_input,
            section_index,
            valid_mask,
            local,
            summed_loss,
        )
        partial_sums = jnp.stack(
            [
                jnp.sum(output_gradient * normalized_input, axis=0),
                jnp.sum(output_gradient, axis=0),
                extra_state,
            ]
        )
        total_counts = lax.psum(partial_sums, "dp")
        norm_sum = norm_sum + jnp.where(valid_mask, total_counts, 0.0)
        preactivation_gradient = (
            norm_gains[0]
            * norm_statistics[1]
            * (
                output_gradient
                - total_counts[1] / counted_rows
                - normalized_input * total_counts[0] / counted_rows
            )
        )
        message, local, piece = lax.switch(
            relay_section,
            [end_reduce, end_conv, end_expand, end_head],
            preactivation_gradient,
            output_gradient,
            section_index,
            valid_mask,
            local,
        )
        gradient_list = local
        grad_in = place(grad_in, section_index, piece, valid_mask)
        return (message, gradient_list, grad_in, norm_sum, summed_loss)

    grad_width = BOTTLENECK_WIDTH
    begin = (
        blank_message,
        jnp.zeros((packed.shape[0], grad_width), jnp.float32),
        jnp.zeros((micro, cells, D), jnp.float32),
        jnp.zeros((3, D), jnp.float32),
        jnp.zeros((), jnp.float32),
    )
    message, gradient_list, grad_in, norm_sum, summed_loss = lax.fori_loop(
        0, micro + 3, backward_tick, begin
    )
    weight_sum = lax.psum_scatter(gradient_list[None], "dp", scatter_dimension=2, tiled=True)
    loss = lax.psum(jnp.where(relay_section == 3, summed_loss, 0.0), ("section", "dp"))
    grad_input = lax.psum_scatter(
        grad_in.reshape(image.shape).astype(jnp.bfloat16),
        "section",
        scatter_dimension=5,
        tiled=True,
    ).astype(jnp.float32)
    return (loss, grad_input, weight_sum, norm_sum[None])


def solution(mesh):
    in_specs = (
        P(None, None, "dp", None, None, None),
        P("section", None, None),
        P("section", None, None),
        P(None, "dp", None),
        P(None, "dp"),
    )
    out_specs = (
        P(),
        P(None, None, "dp", None, None, "section"),
        P("section", None, "dp"),
        P("section", None, None),
    )
    return jax.shard_map(body, mesh=mesh, in_specs=in_specs, out_specs=out_specs, check_vma=False)
```

profile of v0, /device:TPU:2, one launch (start us, length us, event | category | flops | bytes accessed | tf_op | source)
XLA Modules:
  0.0 2340.0 jit_solution(3119974832089595474)
XLA Ops:
  60.4 800.9 %while.54 = (s32[]{:T(128)}, bf16[392,512]{1,0:T(8,128)(2,1)}, f32[2,392,2048]{2,1,0:T(8,128)}, bf16[2,392,512]{2,1,0:T(8,128)(2,1)}, f32[2,2,2048]{2,1,0:T(2,12...) while((s32[]{:T(128)}, bf16[392,512]{1,0:T(8,128)(2,1)}, ...), condition=%wide.region_23.24_spmd, body=%wide.region_0.23_spmd.sunk | while | flops 1878722816 | bytes 168287072 | solution.py:196
  94.4 27.9 %psum.75 = f32[2,2048]{1,0:T(2,128)S(1)} all-reduce(f32[2,2048]{1,0:T(2,128)S(1)} %pad_maximum_fusion.5), channel_id=1, replica_groups=mesh['section'=4,'dp'=8] {'dp'}, use_global_device_ids=true, to_apply=%region_7.7 | all-reduce | flops 4096 | bytes 32768 | tf_op jit(solution)/shard_map/while/body/eval_jaxpr/psum | solution.py:165
  128.4 26.0 %psum.76 = f32[2,3000]{1,0:T(2,128)S(1)} all-reduce(f32[2,3000]{1,0:T(2,128)S(1)} %fusion.170), channel_id=1, replica_groups=mesh['section'=4,'dp'=8] {'dp'}, use_global_device_ids=true, to_apply=%region_15.15 | all-reduce | flops 6000 | bytes 48000 | tf_op jit(solution)/shard_map/while/body/eval_jaxpr/psum | solution.py:44
  158.5 26.0 %psum.77 = f32[2,3000]{1,0:T(2,128)S(1)} all-reduce(f32[2,3000]{1,0:T(2,128)S(1)} %get-tuple-element.1830), channel_id=1, replica_groups=mesh['section'=4,'dp'=8] {'dp'}, use_global_device_ids=true, to_apply=%region_18.18 | all-reduce | flops 6000 | bytes 48000 | tf_op jit(solution)/shard_map/while/body/eval_jaxpr/psum | solution.py:44
  255.2 26.8 %psum.75 = f32[2,2048]{1,0:T(2,128)S(1)} all-reduce(f32[2,2048]{1,0:T(2,128)S(1)} %pad_maximum_fusion.5), channel_id=1, replica_groups=mesh['section'=4,'dp'=8] {'dp'}, use_global_device_ids=true, to_apply=%region_7.7 | all-reduce | flops 4096 | bytes 32768 | tf_op jit(solution)/shard_map/while/body/eval_jaxpr/psum | solution.py:165
  288.0 26.0 %psum.76 = f32[2,3000]{1,0:T(2,128)S(1)} all-reduce(f32[2,3000]{1,0:T(2,128)S(1)} %fusion.170), channel_id=1, replica_groups=mesh['section'=4,'dp'=8] {'dp'}, use_global_device_ids=true, to_apply=%region_15.15 | all-reduce | flops 6000 | bytes 48000 | tf_op jit(solution)/shard_map/while/body/eval_jaxpr/psum | solution.py:44
  318.1 26.0 %psum.77 = f32[2,3000]{1,0:T(2,128)S(1)} all-reduce(f32[2,3000]{1,0:T(2,128)S(1)} %get-tuple-element.1830), channel_id=1, replica_groups=mesh['section'=4,'dp'=8] {'dp'}, use_global_device_ids=true, to_apply=%region_18.18 | all-reduce | flops 6000 | bytes 48000 | tf_op jit(solution)/shard_map/while/body/eval_jaxpr/psum | solution.py:44
  415.4 26.8 %psum.75 = f32[2,2048]{1,0:T(2,128)S(1)} all-reduce(f32[2,2048]{1,0:T(2,128)S(1)} %pad_maximum_fusion.5), channel_id=1, replica_groups=mesh['section'=4,'dp'=8] {'dp'}, use_global_device_ids=true, to_apply=%region_7.7 | all-reduce | flops 4096 | bytes 32768 | tf_op jit(solution)/shard_map/while/body/eval_jaxpr/psum | solution.py:165
  478.4 26.0 %psum.77 = f32[2,3000]{1,0:T(2,128)S(1)} all-reduce(f32[2,3000]{1,0:T(2,128)S(1)} %get-tuple-element.1830), channel_id=1, replica_groups=mesh['section'=4,'dp'=8] {'dp'}, use_global_device_ids=true, to_apply=%region_18.18 | all-reduce | flops 6000 | bytes 48000 | tf_op jit(solution)/shard_map/while/body/eval_jaxpr/psum | solution.py:44
  575.7 26.8 %psum.75 = f32[2,2048]{1,0:T(2,128)S(1)} all-reduce(f32[2,2048]{1,0:T(2,128)S(1)} %pad_maximum_fusion.5), channel_id=1, replica_groups=mesh['section'=4,'dp'=8] {'dp'}, use_global_device_ids=true, to_apply=%region_7.7 | all-reduce | flops 4096 | bytes 32768 | tf_op jit(solution)/shard_map/while/body/eval_jaxpr/psum | solution.py:165
  608.5 26.0 %psum.76 = f32[2,3000]{1,0:T(2,128)S(1)} all-reduce(f32[2,3000]{1,0:T(2,128)S(1)} %fusion.170), channel_id=1, replica_groups=mesh['section'=4,'dp'=8] {'dp'}, use_global_device_ids=true, to_apply=%region_15.15 | all-reduce | flops 6000 | bytes 48000 | tf_op jit(solution)/shard_map/while/body/eval_jaxpr/psum | solution.py:44
  736.0 26.8 %psum.75 = f32[2,2048]{1,0:T(2,128)S(1)} all-reduce(f32[2,2048]{1,0:T(2,128)S(1)} %pad_maximum_fusion.5), channel_id=1, replica_groups=mesh['section'=4,'dp'=8] {'dp'}, use_global_device_ids=true, to_apply=%region_7.7 | all-reduce | flops 4096 | bytes 32768 | tf_op jit(solution)/shard_map/while/body/eval_jaxpr/psum | solution.py:165
  798.9 26.0 %psum.77 = f32[2,3000]{1,0:T(2,128)S(1)} all-reduce(f32[2,3000]{1,0:T(2,128)S(1)} %get-tuple-element.1830), channel_id=1, replica_groups=mesh['section'=4,'dp'=8] {'dp'}, use_global_device_ids=true, to_apply=%region_18.18 | all-reduce | flops 6000 | bytes 48000 | tf_op jit(solution)/shard_map/while/body/eval_jaxpr/psum | solution.py:44
  869.0 603.2 %while.55 = (s32[]{:T(128)}, bf16[392,512]{1,0:T(8,128)(2,1)}, f32[9456,512]{1,0:T(8,128)}, bf16[2,392,2048]{2,1,0:T(8,128)(2,1)}, f32[3,2048]{1,0:T(4,128)S(1)}...) while((s32[]{:T(128)}, bf16[392,512]{1,0:T(8,128)(2,1)}, ...), condition=%wide.region_46.47_spmd.clone, body=%wide.region_24.46_spmd.clone.sunk | while | flops 3747306752 | bytes 224168176 | solution.py:411
  911.0 27.5 %psum.79 = f32[3,2048]{1,0:T(4,128)S(1)} all-reduce(f32[3,2048]{1,0:T(4,128)S(1)} %pad_maximum_fusion.6), channel_id=1, replica_groups=mesh['section'=4,'dp'=8] {'dp'}, use_global_device_ids=true, to_apply=%region_41.41 | all-reduce | flops 6144 | bytes 49152 | tf_op jit(solution)/shard_map/while/body/eval_jaxpr/psum | solution.py:379
  942.4 46.4 %conditional.13 = (bf16[392,512]{1,0:T(8,128)(2,1)}, f32[9456,512]{1,0:T(8,128)}, f32[392,2048]{1,0:T(8,128)S(1)}) conditional(s32[]{:T(128)} %get-tuple-element.2045, (f32[9456,512]{1,0:T(8,128)}, pred[]{:T(512)}, s32[]{:T(128)}, bf16[2,2,4,7,7,2048]{5,4,3,2,1,0:T(8,128)(2,1)}, bf16[392,2048]{1,0:T(8,128)(2,1)}, ...), branch_computations={%region_42.42_spmd, %region_43.43_spmd, %region_44.44_spmd, %regio... | conditional | flops 3706294272 | bytes 144597312 | solution.py:390
  1007.3 27.5 %psum.79 = f32[3,2048]{1,0:T(4,128)S(1)} all-reduce(f32[3,2048]{1,0:T(4,128)S(1)} %pad_maximum_fusion.6), channel_id=1, replica_groups=mesh['section'=4,'dp'=8] {'dp'}, use_global_device_ids=true, to_apply=%region_41.41 | all-reduce | flops 6144 | bytes 49152 | tf_op jit(solution)/shard_map/while/body/eval_jaxpr/psum | solution.py:379
  1038.8 46.3 %conditional.13 = (bf16[392,512]{1,0:T(8,128)(2,1)}, f32[9456,512]{1,0:T(8,128)}, f32[392,2048]{1,0:T(8,128)S(1)}) conditional(s32[]{:T(128)} %get-tuple-element.2045, (f32[9456,512]{1,0:T(8,128)}, pred[]{:T(512)}, s32[]{:T(128)}, bf16[2,2,4,7,7,2048]{5,4,3,2,1,0:T(8,128)(2,1)}, bf16[392,2048]{1,0:T(8,128)(2,1)}, ...), branch_computations={%region_42.42_spmd, %region_43.43_spmd, %region_44.44_spmd, %regio... | conditional | flops 3706294272 | bytes 144597312 | solution.py:390
  1126.8 27.5 %psum.79 = f32[3,2048]{1,0:T(4,128)S(1)} all-reduce(f32[3,2048]{1,0:T(4,128)S(1)} %pad_maximum_fusion.6), channel_id=1, replica_groups=mesh['section'=4,'dp'=8] {'dp'}, use_global_device_ids=true, to_apply=%region_41.41 | all-reduce | flops 6144 | bytes 49152 | tf_op jit(solution)/shard_map/while/body/eval_jaxpr/psum | solution.py:379
  1158.2 46.3 %conditional.13 = (bf16[392,512]{1,0:T(8,128)(2,1)}, f32[9456,512]{1,0:T(8,128)}, f32[392,2048]{1,0:T(8,128)S(1)}) conditional(s32[]{:T(128)} %get-tuple-element.2045, (f32[9456,512]{1,0:T(8,128)}, pred[]{:T(512)}, s32[]{:T(128)}, bf16[2,2,4,7,7,2048]{5,4,3,2,1,0:T(8,128)(2,1)}, bf16[392,2048]{1,0:T(8,128)(2,1)}, ...), branch_computations={%region_42.42_spmd, %region_43.43_spmd, %region_44.44_spmd, %regio... | conditional | flops 3706294272 | bytes 144597312 | solution.py:390
  1216.2 34.7 %collective-permute-done.1 = bf16[392,512]{1,0:T(8,128)(2,1)} collective-permute-done((bf16[392,512]{1,0:T(8,128)(2,1)}, bf16[392,512]{1,0:T(8,128)(2,1)}, u32[]{:S(2)}, u32[]{:S(2)}) %collective-permute-start.1) | collective-permute-done | bytes 401440 | tf_op jit(solution)/shard_map/while/body/eval_jaxpr/ppermute | solution.py:24
  1255.3 27.5 %psum.79 = f32[3,2048]{1,0:T(4,128)S(1)} all-reduce(f32[3,2048]{1,0:T(4,128)S(1)} %pad_maximum_fusion.6), channel_id=1, replica_groups=mesh['section'=4,'dp'=8] {'dp'}, use_global_device_ids=true, to_apply=%region_41.41 | all-reduce | flops 6144 | bytes 49152 | tf_op jit(solution)/shard_map/while/body/eval_jaxpr/psum | solution.py:379
  1286.8 46.3 %conditional.13 = (bf16[392,512]{1,0:T(8,128)(2,1)}, f32[9456,512]{1,0:T(8,128)}, f32[392,2048]{1,0:T(8,128)S(1)}) conditional(s32[]{:T(128)} %get-tuple-element.2045, (f32[9456,512]{1,0:T(8,128)}, pred[]{:T(512)}, s32[]{:T(128)}, bf16[2,2,4,7,7,2048]{5,4,3,2,1,0:T(8,128)(2,1)}, bf16[392,2048]{1,0:T(8,128)(2,1)}, ...), branch_computations={%region_42.42_spmd, %region_43.43_spmd, %region_44.44_spmd, %regio... | conditional | flops 3706294272 | bytes 144597312 | solution.py:390
  1344.7 34.7 %collective-permute-done.1 = bf16[392,512]{1,0:T(8,128)(2,1)} collective-permute-done((bf16[392,512]{1,0:T(8,128)(2,1)}, bf16[392,512]{1,0:T(8,128)(2,1)}, u32[]{:S(2)}, u32[]{:S(2)}) %collective-permute-start.1) | collective-permute-done | bytes 401440 | tf_op jit(solution)/shard_map/while/body/eval_jaxpr/ppermute | solution.py:24
  1383.8 27.5 %psum.79 = f32[3,2048]{1,0:T(4,128)S(1)} all-reduce(f32[3,2048]{1,0:T(4,128)S(1)} %pad_maximum_fusion.6), channel_id=1, replica_groups=mesh['section'=4,'dp'=8] {'dp'}, use_global_device_ids=true, to_apply=%region_41.41 | all-reduce | flops 6144 | bytes 49152 | tf_op jit(solution)/shard_map/while/body/eval_jaxpr/psum | solution.py:379
  1415.3 46.3 %conditional.13 = (bf16[392,512]{1,0:T(8,128)(2,1)}, f32[9456,512]{1,0:T(8,128)}, f32[392,2048]{1,0:T(8,128)S(1)}) conditional(s32[]{:T(128)} %get-tuple-element.2045, (f32[9456,512]{1,0:T(8,128)}, pred[]{:T(512)}, s32[]{:T(128)}, bf16[2,2,4,7,7,2048]{5,4,3,2,1,0:T(8,128)(2,1)}, bf16[392,2048]{1,0:T(8,128)(2,1)}, ...), branch_computations={%region_42.42_spmd, %region_43.43_spmd, %region_44.44_spmd, %regio... | conditional | flops 3706294272 | bytes 144597312 | solution.py:390
  1477.5 322.5 %copy.51 = bf16[2,2,4,7,7,2048]{0,4,3,2,1,5:T(8,128)(2,1)} copy(bf16[2,2,4,7,7,2048]{5,0,4,3,2,1:T(2,128)(2,1)S(1)} %bitcast.326) | data formatting | bytes 6422528
  1800.0 213.8 %reshape.445 = bf16[2048,784]{1,0:T(8,128)(2,1)} reshape(bf16[2048,2,4,7,7,2]{5,4,3,2,1,0:T(8,128)(2,1)} %bitcast.103) | data formatting | bytes 6422528
  2033.7 114.9 %psum.68 = f32[]{:T(128)} all-reduce(f32[]{:T(128)S(6)} %select_n.244), channel_id=1, replica_groups=mesh['section'=4,'dp'=8] {'section','dp'}, use_global_device_ids=true, to_apply=%region_47.48 | all-reduce | flops 1 | bytes 8 | tf_op jit(solution)/shard_map/psum | solution.py:415
  2149.2 59.7 %reshape.446 = bf16[512,2,4,7,7,2]{5,4,3,2,1,0:T(8,128)(2,1)} reshape(bf16[512,784]{1,0:T(8,128)(2,1)} %reduce-scatter.7.cloned.1.call-done) | data formatting | bytes 1605632
  2208.9 57.0 %copy.52 = bf16[2,2,4,7,7,512]{5,0,4,3,2,1:T(2,128)(2,1)S(1)} copy(bf16[2,2,4,7,7,512]{0,4,3,2,1,5:T(8,128)(2,1)} %bitcast.324) | data formatting | bytes 1605632
  2267.4 65.5 %reduce-scatter.5.cloned.1.call-done = f32[1,9456,64]{1,2,0:T(8,128)} async-done(((f32[1,9456,512]{1,2,0:T(8,128)}), f32[1,9456,64]{1,2,0:T(8,128)}) %reduce-scatter.5.cloned.1.call-update) | async-done | bytes 2420752 | tf_op jit(solution)/shard_map/reduce_scatter | solution.py:414
  (838 shorter events, 1049.3 us)
Async XLA Ops:
  7.2 44.4 %copy-start = (bf16[2,64,128]{2,1,0:T(8,128)(2,1)S(1)}, bf16[2,64,128]{2,1,0:T(8,128)(2,1)}, u32[]{:S(2)}) copy-start(bf16[2,64,128]{2,1,0:T(8,128)(2,1)} %param.40) | copy-start | bytes 98308
  7.2 2142.0 %reduce-scatter.7.cloned.1.call-start = ((), (), s32[]{:S(2)}) async-start(), calls=%async_computation.3 | async-start | bytes 4587520
  37.5 14.0 copy-start.31
  60.8 63.7 %copy-start.25 = (f32[3,2048]{1,0:T(4,128)}, f32[3,2048]{1,0:T(4,128)S(1)}, u32[]{:S(2)}) copy-start(f32[3,2048]{1,0:T(4,128)S(1)} %get-tuple-element.1968) | copy-start | bytes 73732 | tf_op jit(solution)/shard_map/while
  60.8 13.1 collective-permute-start
  74.7 10.5 copy-start.9
  220.9 63.3 %copy-start.25 = (f32[3,2048]{1,0:T(4,128)}, f32[3,2048]{1,0:T(4,128)S(1)}, u32[]{:S(2)}) copy-start(f32[3,2048]{1,0:T(4,128)S(1)} %get-tuple-element.1968) | copy-start | bytes 73732 | tf_op jit(solution)/shard_map/while
  220.9 13.9 collective-permute-start
  235.5 10.5 copy-start.9
  380.5 63.8 %copy-start.25 = (f32[3,2048]{1,0:T(4,128)}, f32[3,2048]{1,0:T(4,128)S(1)}, u32[]{:S(2)}) copy-start(f32[3,2048]{1,0:T(4,128)S(1)} %get-tuple-element.1968) | copy-start | bytes 73732 | tf_op jit(solution)/shard_map/while
  380.5 14.4 collective-permute-start
  395.7 10.5 copy-start.9
  540.8 63.8 %copy-start.25 = (f32[3,2048]{1,0:T(4,128)}, f32[3,2048]{1,0:T(4,128)S(1)}, u32[]{:S(2)}) copy-start(f32[3,2048]{1,0:T(4,128)S(1)} %get-tuple-element.1968) | copy-start | bytes 73732 | tf_op jit(solution)/shard_map/while
  540.8 14.4 collective-permute-start
  555.9 10.5 copy-start.9
  701.0 63.8 %copy-start.25 = (f32[3,2048]{1,0:T(4,128)}, f32[3,2048]{1,0:T(4,128)S(1)}, u32[]{:S(2)}) copy-start(f32[3,2048]{1,0:T(4,128)S(1)} %get-tuple-element.1968) | copy-start | bytes 73732 | tf_op jit(solution)/shard_map/while
  701.0 14.4 collective-permute-start
  716.2 10.5 copy-start.9
  892.7 13.9 copy-start.27
  892.7 13.9 collective-permute-start.1
  956.9 8.0 copy-start.13
  991.9 11.0 copy-start.27
  991.9 11.0 collective-permute-start.1
  1088.2 34.1 %copy-start.27 = (f32[3,2048]{1,0:T(4,128)}, f32[3,2048]{1,0:T(4,128)S(1)}, u32[]{:S(2)}) copy-start(f32[3,2048]{1,0:T(4,128)S(1)} %get-tuple-element.2035) | copy-start | bytes 73732 | tf_op jit(solution)/shard_map/while
  1088.2 34.1 %collective-permute-start.1 = (bf16[392,512]{1,0:T(8,128)(2,1)}, bf16[392,512]{1,0:T(8,128)(2,1)}, u32[]{:S(2)}, u32[]{:S(2)}) collective-permute-start(bf16[392,512]{1,0:T(8,128)(2,1)} %get-tuple-element.2003), channel_id=1, source_target_pairs={{8,0},{16,8},{24,16},{9,1},{17,9},{25,17},{10,2},{18,10},{26,18},{... | collective-permute-start | bytes 1204232 | tf_op jit(solution)/shard_map/while/body/eval_jaxpr/ppermute | solution.py:24
  1207.7 43.2 %copy-start.27 = (f32[3,2048]{1,0:T(4,128)}, f32[3,2048]{1,0:T(4,128)S(1)}, u32[]{:S(2)}) copy-start(f32[3,2048]{1,0:T(4,128)S(1)} %get-tuple-element.2035) | copy-start | bytes 73732 | tf_op jit(solution)/shard_map/while
  1207.7 43.2 %collective-permute-start.1 = (bf16[392,512]{1,0:T(8,128)(2,1)}, bf16[392,512]{1,0:T(8,128)(2,1)}, u32[]{:S(2)}, u32[]{:S(2)}) collective-permute-start(bf16[392,512]{1,0:T(8,128)(2,1)} %get-tuple-element.2003), channel_id=1, source_target_pairs={{8,0},{16,8},{24,16},{9,1},{17,9},{25,17},{10,2},{18,10},{26,18},{... | collective-permute-start | bytes 1204232 | tf_op jit(solution)/shard_map/while/body/eval_jaxpr/ppermute | solution.py:24
  1336.2 43.2 %copy-start.27 = (f32[3,2048]{1,0:T(4,128)}, f32[3,2048]{1,0:T(4,128)S(1)}, u32[]{:S(2)}) copy-start(f32[3,2048]{1,0:T(4,128)S(1)} %get-tuple-element.2035) | copy-start | bytes 73732 | tf_op jit(solution)/shard_map/while
  1336.2 43.2 %collective-permute-start.1 = (bf16[392,512]{1,0:T(8,128)(2,1)}, bf16[392,512]{1,0:T(8,128)(2,1)}, u32[]{:S(2)}, u32[]{:S(2)}) collective-permute-start(bf16[392,512]{1,0:T(8,128)(2,1)} %get-tuple-element.2003), channel_id=1, source_target_pairs={{8,0},{16,8},{24,16},{9,1},{17,9},{25,17},{10,2},{18,10},{26,18},{... | collective-permute-start | bytes 1204232 | tf_op jit(solution)/shard_map/while/body/eval_jaxpr/ppermute | solution.py:24
  2013.9 319.1 %reduce-scatter.5.cloned.1.call-start = ((), (), s32[]{:S(2)}) async-start(), calls=%async_computation.2 | async-start | bytes 21823488 | tf_op jit(solution)/shard_map/reduce_scatter | solution.py:414
  2033.7 114.9 %copy-start.34 = (f32[3,2048]{1,0:T(4,128)S(1)}, f32[3,2048]{1,0:T(4,128)}, u32[]{:S(2)}) copy-start(f32[3,2048]{1,0:T(4,128)} %copy-done.33) | copy-start | bytes 73732
  2208.9 124.0 %copy-start.1 = (bf16[2,64,128]{2,1,0:T(8,128)(2,1)S(1)}, bf16[2,64,128]{2,1,0:T(8,128)(2,1)}, u32[]{:S(2)}) copy-start(bf16[2,64,128]{2,1,0:T(8,128)(2,1)} %param.40) | copy-start | bytes 98308
  (123 other events, 409.3 us)
Sparse Core Ops, SparseCore 0:
  2014.0 122.9 reduce-scatter.6
  2139.9 192.9 reduce-scatter.4
where the time goes:
time: 2360 us; the launch traced here: 2340 us
  local copies, waits for them, and re-layouts  923 us (39%)
  blocking collectives  777 us (33%)
  other arithmetic  266 us (11%)
  waiting for transfers between devices  172 us (7%)
  matrix products  110 us (5%)
  starting transfers between devices  43.4 us (2%)
  loops' own time  35.5 us (2%)
    unnamed x20, local copies, waits for them, and re-layouts  655 us
    psum x15, blocking collectives, balance_each(): column = lax.psum(jnp.sum(mass, axis=1), 'dp')  389 us
    psum x5, blocking collectives, backward_tick(): total_counts = lax.psum(partial_sums, 'dp')  137 us
    psum x5, blocking collectives, forward_tick(): norm_statistics = lax.psum(partial_sums, 'dp')  135 us
    psum x1, blocking collectives, body(): lax.psum(jnp.where(relay_section == 3, summed_loss, 0.0), ('section', 'dp'))  115 us
    ppermute x10, waiting for transfers between devices, shifted(): lax.ppermute(value, axis, [(source, source + steps) for source in range(f...  106 us
    reshape x80, local copies, waits for them, and re-layouts, taps_of(): grid[:, tap // 3:tap // 3 + SIDE, tap % 3:tap % 3 + SIDE]  71.2 us
    reduce_scatter x1, waiting for transfers between devices, body(): lax.psum_scatter(gradient_list[None], 'dp', scatter_dimension=2, tiled=True)  65.5 us
  transfers between devices with their start and end apart: 12, of which 7 were waited for; matrix products, arithmetic and copies ran while one was open for 9% of the time, Pallas kernels for 0%

commit v1 on v0

v1 whole, which is shorter than its diff:
```python
import functools

import jax
import jax.numpy as jnp
from jax import lax
from jax.experimental import pallas as pl
from jax.experimental.pallas import tpu as pltpu
from jax.sharding import PartitionSpec as P

D = 2048
WIDTH = 512
PROJ = 128
PROTOS = 3000
SIDE = 7
CROPS = 2
SECTIONS = 4
PART = WIDTH // SECTIONS
WIDE = D // SECTIONS
QUARTER = PROTOS // 4
QUARTER_PAD = 768
PLACES = SIDE * SIDE
FIRST = D * (D // WIDTH)
SECOND = FIRST + D * PROJ // WIDTH
THIRD = SECOND + PROTOS * PROJ // WIDTH

NORM_EPS = 1e-05
UNIT_EPS = 1e-06
SINK_EPS = 0.05
TEMPER = 0.1
HIGH = lax.Precision.HIGHEST
F32 = jnp.float32
BF16 = jnp.bfloat16
NT = (((1,), (1,)), ((), ()))
TN = (((0,), (0,)), ((), ()))


def dot(a, b):
    return jnp.dot(a, b, preferred_element_type=F32)


def dot_nt(a, b):
    return lax.dot_general(a, b, NT, preferred_element_type=F32)


def dot_tn(a, b):
    return lax.dot_general(a, b, TN, preferred_element_type=F32)


def flip(value, axis, step):
    count = lax.axis_size(axis)
    return lax.ppermute(value, axis, [(source, source ^ step) for source in range(count)])


def send(value, source, target):
    return lax.ppermute(value, "section", [(source, target)])


def sum_dp(value):
    count = lax.axis_size("dp")
    value = value + flip(value, "dp", 1)
    step = 2
    while step < count:
        if 2 * step < count:
            near = value + flip(value, "dp", step)
            far = flip(value, "dp", 2 * step) + flip(value, "dp", 3 * step)
            value = near + far
            step *= 4
        else:
            value = value + flip(value, "dp", step)
            step *= 2
    return value


def gather_xor(value, axis):
    return [value] + [flip(value, axis, step) for step in range(1, lax.axis_size(axis))]


def gather_dp(value):
    count = lax.axis_size("dp")
    value = jnp.stack([value, flip(value, "dp", 1)])
    step = 2
    while step < count:
        if 2 * step < count:
            value = jnp.concatenate(
                [value] + [flip(value, "dp", step * j) for j in (1, 2, 3)]
            )
            step *= 4
        else:
            value = jnp.concatenate([value, flip(value, "dp", step)])
            step *= 2
    return value


def sigmoid(v):
    return 1.0 / (1.0 + jnp.exp(-v))


def slope(v):
    s = sigmoid(v)
    return s * (1.0 + v * (1.0 - s))


def call(kernel, out, *args, scratch=(), vmem=32):
    in_specs = []
    for a in args:
        if jnp.issubdtype(a.dtype, jnp.integer):
            in_specs.append(pl.BlockSpec(memory_space=pltpu.SMEM))
        else:
            in_specs.append(pl.BlockSpec(memory_space=pltpu.VMEM))
    return pl.pallas_call(
        kernel,
        out_shape=out,
        in_specs=in_specs,
        out_specs=jax.tree.map(lambda _: pl.BlockSpec(memory_space=pltpu.VMEM), out),
        scratch_shapes=list(scratch),
        compiler_params=pltpu.CompilerParams(vmem_limit_bytes=vmem * 2**20),
    )(*args)


def shape(dims, dtype):
    return jax.ShapeDtypeStruct(tuple(dims), dtype)


def split_sums(first, second, micro):
    width = first[0].shape[1]
    rows = [jnp.sum(v, axis=0, keepdims=True) for v in first]
    rows += [jnp.sum(v, axis=0, keepdims=True) for v in second]
    rows.append(jnp.zeros((8 - 2 * micro, width), F32))
    return jnp.concatenate(rows, axis=0)


def moments(sums, m, micro, count):
    mean = sums[m : m + 1] * (1.0 / count)
    square = sums[micro + m : micro + m + 1] * (1.0 / count)
    return mean, lax.rsqrt(square - mean * mean + NORM_EPS)


def per_micro(value, micro):
    rows = value.shape[0] // micro
    return [value[m * rows : (m + 1) * rows] for m in range(micro)]


def normalized(value, sums, micro, count):
    out = []
    for m, v in enumerate(per_micro(value, micro)):
        mean, rstd = moments(sums, m, micro, count)
        out.append(((v - mean) * rstd, rstd))
    return out


def join(parts):
    return jnp.concatenate(parts, axis=0)


def tap_valid(rows, images, tap, sign):
    row = lax.broadcasted_iota(jnp.int32, (rows, PART), 0).astype(F32)
    cell = jnp.floor((row + 0.5) * (1.0 / images))
    crop = jnp.floor((cell + 0.5) * (1.0 / PLACES))
    place = cell - crop * PLACES
    y = jnp.floor((place + 0.5) * (1.0 / SIDE))
    x = place - y * SIDE
    y = y + float(sign * (tap // 3 - 1))
    x = x + float(sign * (tap % 3 - 1))
    return (y > -0.5) & (y < SIDE - 0.5) & (x > -0.5) & (x < SIDE - 0.5)


def tap_shift(value, images, tap, sign):
    rows = value.shape[0]
    offset = sign * images * (SIDE * (tap // 3 - 1) + (tap % 3 - 1))
    moved = value if offset == 0 else pltpu.roll(value, (-offset) % rows, 0)
    if tap == 4:
        return moved
    return jnp.where(tap_valid(rows, images, tap, sign), moved, 0.0)


def reduce_kernel(micro, image, weight, pre, sums):
    value = dot(image[...], weight[...])
    pre[...] = value.astype(BF16)
    parts = per_micro(value, micro)
    sums[...] = split_sums(parts, [v * v for v in parts], micro)


def fill_active(micro, count, place, pieces, sums, norm, full, own=None):
    for k, piece in enumerate(pieces):
        lanes = pl.ds(pl.multiple_of(place[k] * PART, PART), PART)
        gain = norm[0:1, lanes]
        shift = norm[1:2, lanes]
        out = []
        for xhat, _ in normalized(piece[...].astype(F32), sums[k], micro, count):
            y = xhat * gain + shift
            out.append(y * sigmoid(y))
        value = join(out).astype(BF16)
        full[:, lanes] = value
        if k == 0 and own is not None:
            own[...] = value


def conv_kernel(micro, images, count, place, p0, p1, p2, p3, sums, norm, weight, own, pre, sums_out, full):
    fill_active(micro, count, place, (p0, p1, p2, p3), sums, norm, full, own)
    active = full[...]
    total = None
    for tap in range(9):
        part = dot(active, weight[tap * WIDTH : (tap + 1) * WIDTH, :])
        part = tap_shift(part, images, tap, 1)
        total = part if total is None else total + part
    pre[...] = total.astype(BF16)
    parts = per_micro(total, micro)
    sums_out[...] = split_sums(parts, [v * v for v in parts], micro)


def expand_kernel(micro, count, place, p0, p1, p2, p3, sums, norm, weight, active, pre, sums_out):
    fill_active(micro, count, place, (p0, p1, p2, p3), sums, norm, active)
    value = dot(active[...], weight[...])
    pre[...] = value
    parts = per_micro(value, micro)
    sums_out[...] = split_sums(parts, [v * v for v in parts], micro)


def crop_rows(rows, images, transpose=False):
    shp = (rows // PLACES, rows)
    r = lax.broadcasted_iota(jnp.int32, shp, 1).astype(F32)
    q = lax.broadcasted_iota(jnp.int32, shp, 0).astype(F32)
    cell = jnp.floor((r + 0.5) * (1.0 / images))
    crop = jnp.floor((cell + 0.5) * (1.0 / PLACES))
    image = r - cell * images
    return (jnp.abs(crop * images + image - q) < 0.5).astype(F32).astype(BF16)


def pool_kernel(micro, images, count, place, pre, sums, norm, image, pooled):
    lanes = pl.ds(pl.multiple_of(place[0] * WIDE, WIDE), WIDE)
    out = []
    for xhat, _ in normalized(pre[...], sums[...], micro, count):
        out.append(xhat * norm[0:1, :] + norm[1:2, :])
    z = join(out) + image[:, lanes].astype(F32)
    out = z * sigmoid(z)
    high = out.astype(BF16)
    low = (out - high.astype(F32)).astype(BF16)
    choose = crop_rows(pre.shape[0], images)
    pooled[...] = ((dot(choose, high) + dot(choose, low)) * (1.0 / PLACES)).astype(BF16)


def out_back_kernel(micro, images, count, place, pre, sums, norm, image, d_pooled, d_z, sums_out):
    lanes = pl.ds(pl.multiple_of(place[0] * WIDE, WIDE), WIDE)
    rows = pre.shape[0]
    spread = dot_tn(crop_rows(rows, images), d_pooled[...]) * (1.0 / PLACES)
    xhats = [x for x, _ in normalized(pre[...], sums[...], micro, count)]
    z = join([x * norm[0:1, :] + norm[1:2, :] for x in xhats]) + image[:, lanes].astype(F32)
    value = spread * slope(z)
    d_z[...] = value
    parts = per_micro(value, micro)
    sums_out[...] = split_sums([v * x for v, x in zip(parts, xhats)], parts, micro)


def norm_back(value, pre, sums, back, gain, micro, count):
    out = []
    parts = per_micro(value, micro)
    for m, (xhat, rstd) in enumerate(normalized(pre, sums, micro, count)):
        by_x = back[m : m + 1] * (1.0 / count)
        plain = back[micro + m : micro + m + 1] * (1.0 / count)
        out.append(gain * rstd * (parts[m] - plain - xhat * by_x))
    return join(out)


def expand_back_kernel(micro, count, place, pre, sums, norm, d_z, back, weight, d_pre, q0, q1, q2, q3, full):
    d_low = norm_back(d_z[...], pre[...], sums[...], back[...], norm[0:1, :], micro, count).astype(BF16)
    d_pre[...] = d_low
    full[...] = dot_nt(d_low, weight[...])
    for k, q in enumerate((q0, q1, q2, q3)):
        lanes = pl.ds(pl.multiple_of(place[k] * PART, PART), PART)
        q[...] = full[:, lanes].astype(BF16)


def silu_back_kernel(micro, count, place, q0, q1, q2, q3, pre, sums, norm, d_y, sums_out):
    total = (q0[...].astype(F32) + q1[...].astype(F32)) + (q2[...].astype(F32) + q3[...].astype(F32))
    d_active = total.astype(BF16).astype(F32)
    finish_silu(micro, count, place, d_active, pre, sums, norm, d_y, sums_out)


def finish_silu(micro, count, place, d_active, pre, sums, norm, d_y, sums_out):
    lanes = pl.ds(pl.multiple_of(place[0] * PART, PART), PART)
    gain = norm[0:1, lanes]
    shift = norm[1:2, lanes]
    values, products = [], []
    parts = per_micro(d_active, micro)
    for m, (xhat, _) in enumerate(normalized(pre[...].astype(F32), sums[0], micro, count)):
        value = parts[m] * slope(xhat * gain + shift)
        values.append(value)
        products.append(value * xhat)
    d_y[...] = join(values).astype(BF16)
    sums_out[...] = split_sums(products, values, micro)


def fill_d_pre(micro, count, place, pieces, backs, pres, sums, norm, full, grads):
    for k, piece in enumerate(pieces):
        lanes = pl.ds(pl.multiple_of(place[k] * PART, PART), PART)
        value = norm_back(
            piece[...].astype(F32), pres[k][...].astype(F32), sums[k], backs[k], norm[0:1, lanes], micro, count
        )
        full[:, lanes] = value.astype(BF16)
        back = backs[k]
        gain = back[0:1]
        shift = back[micro : micro + 1]
        for m in range(1, micro):
            gain = gain + back[m : m + 1]
            shift = shift + back[micro + m : micro + m + 1]
        grads[:, lanes] = join([gain, shift, jnp.zeros((6, PART), F32)])


def conv_back_kernel(
    micro, images, count, place, d0, d1, d2, d3, back, p0, p1, p2, p3, sums, norm, weight, pre, sums0, norm0,
    d_full, grads, d_y, sums_out,
):
    fill_d_pre(micro, count, place, (d0, d1, d2, d3), back, (p0, p1, p2, p3), sums, norm, d_full, grads)
    d_low = d_full[...]
    total = None
    for tap in range(9):
        part = dot_nt(d_low, weight[tap * PART : (tap + 1) * PART, :])
        part = tap_shift(part, images, tap, -1)
        total = part if total is None else total + part
    d_active = total.astype(BF16).astype(F32)
    finish_silu(micro, count, place, d_active, pre, sums0, norm0, d_y, sums_out)


def reduce_back_kernel(
    micro, count, place, d0, d1, d2, d3, back, p0, p1, p2, p3, sums, norm, weight, d_z, d_full, grads, grad_in
):
    fill_d_pre(micro, count, place, (d0, d1, d2, d3), back, (p0, p1, p2, p3), sums, norm, d_full, grads)
    main = dot_nt(d_full[...], weight[...]).astype(BF16).astype(F32)
    grad_in[...] = main + d_z[...].astype(BF16).astype(F32)


def taps_kernel(images, active, out):
    value = active[...].astype(F32)
    for tap in range(9):
        out[:, tap * PART : (tap + 1) * PART] = tap_shift(value, images, tap, 1).astype(BF16)


def head(pooled, w_head, w_proj, protos, norm, queue, match, micro, images, dp):
    rows = pooled.shape[0]
    group = rows // micro
    half = group // CROPS
    scale_all = 1.0 / (TEMPER * CROPS * half * micro)
    pre = dot(pooled, w_head)

    def by_micro(v):
        return v.reshape(micro, group, v.shape[-1])

    pre_m = by_micro(pre)
    mean = jnp.mean(pre_m, axis=1, keepdims=True)
    square = jnp.mean(pre_m * pre_m, axis=1, keepdims=True)
    rstd = lax.rsqrt(square - mean * mean + NORM_EPS)
    xhat = (pre_m - mean) * rstd
    y = xhat * norm[0] + norm[1]
    active = (y * sigmoid(y)).astype(BF16).reshape(rows, D)
    embed = dot(active, w_proj) + norm[2, :PROJ]
    recip = lax.rsqrt(jnp.sum(embed * embed, axis=1, keepdims=True) + UNIT_EPS)
    unit = (embed * recip).astype(BF16)
    scores = dot_nt(unit, protos)
    valid = lax.broadcasted_iota(jnp.int32, (1, 4, QUARTER_PAD), 2).reshape(1, 4 * QUARTER_PAD) < QUARTER
    own_mass = jnp.where(valid, jnp.exp(scores / SINK_EPS), 0.0).reshape(micro, CROPS, half, -1)
    queue_mass = jnp.where(valid, jnp.exp(jnp.einsum("cqp,kp->cqk", queue, protos, preferred_element_type=F32) / SINK_EPS), 0.0)
    codes = []
    for m in range(micro):
        for c in range(CROPS):
            a, b = queue_mass[c], own_mass[m, c]
            column = jnp.sum(a, axis=0, keepdims=True) + jnp.sum(b, axis=0, keepdims=True)
            once = jnp.where(valid, 1.0 / column, 0.0)
            a, b = a * once, b * once
            scale = valid.astype(F32)
            for turn in range(2):
                ra = 1.0 / jnp.sum(a * scale, axis=1, keepdims=True)
                rb = 1.0 / jnp.sum(b * scale, axis=1, keepdims=True)
                column = jnp.sum(a * ra, axis=0, keepdims=True) + jnp.sum(b * rb, axis=0, keepdims=True)
                scale = jnp.where(valid, 1.0 / column, 0.0)
            b = b * scale
            codes.append(b / jnp.sum(b, axis=1, keepdims=True))
    targets = []
    for m in range(micro):
        targets.append(jnp.dot(match[m], codes[m * CROPS + 1], precision=HIGH))
        targets.append(jnp.dot(match[m].T, codes[m * CROPS], precision=HIGH))
    target = jnp.concatenate(targets)
    logits = jnp.where(valid, scores / TEMPER, -1e30)
    logp = jax.nn.log_softmax(logits, axis=1)
    loss = -jnp.sum(jnp.where(valid, target * logp, 0.0)) * (TEMPER * scale_all)
    d_scores = ((jnp.exp(logp) * jnp.sum(target, axis=1, keepdims=True) - target) * scale_all).astype(BF16)
    d_unit = dot(d_scores, protos)
    d_embed = (
        recip * d_unit - embed * (recip * recip * recip) * jnp.sum(d_unit * embed, axis=1, keepdims=True)
    ).astype(BF16)
    d_active = dot_nt(d_embed, w_proj)
    d_y = by_micro(d_active) * slope(y)
    by_x = jnp.sum(d_y * xhat, axis=1, keepdims=True)
    plain = jnp.sum(d_y, axis=1, keepdims=True)
    d_pre = (norm[0] * rstd * (d_y - plain / group - xhat * by_x / group)).astype(BF16).reshape(rows, D)
    bias = jnp.pad(jnp.sum(d_embed.astype(F32), axis=0), (0, D - PROJ))
    grads = jnp.stack([jnp.sum(by_x, axis=(0, 1)), jnp.sum(plain, axis=(0, 1)), bias])
    return loss, grads, active, unit, d_scores, d_embed, d_pre


def interleave(width):
    row = lax.broadcasted_iota(jnp.int32, (4 * width, 4 * width), 0)
    column = lax.broadcasted_iota(jnp.int32, (4 * width, 4 * width), 1)
    return (column == 4 * (row % width) + row // width).astype(BF16)


def head_grads_kernel(pooled, active, unit, d_scores, d_embed, d_pre, choose, weave, out):
    own = choose.shape[1]
    block = PART
    parts = []
    for q in range(4):
        own_d = dot(d_pre[:, q * WIDTH : (q + 1) * WIDTH], choose[...]).astype(BF16)
        parts.append(dot_tn(own_d, pooled[...]).astype(BF16))
    for b in range(D // block):
        mixed = jnp.concatenate([p[:, b * block : (b + 1) * block] for p in parts], axis=1)
        out[:, 4 * block * b : 4 * block * (b + 1)] = dot(mixed, weave[...])
    proj = jnp.zeros((own, WIDTH), F32)
    proto = jnp.zeros((own, QUARTER_PAD), F32)
    apart = []
    for b in range(4):
        apart.append(dot_nt(active[:, b * WIDTH : (b + 1) * WIDTH], weave[...]).astype(BF16))
    for a in range(4):
        some = choose[a * PROJ : (a + 1) * PROJ, :]
        own_e = dot(d_embed[...], some).astype(BF16)
        own_u = dot(unit[...], some).astype(BF16)
        column = jnp.concatenate([v[:, a * block : (a + 1) * block] for v in apart], axis=1)
        proj = proj + dot_tn(own_e, column)
        proto = proto + dot_tn(own_u, d_scores[:, a * QUARTER_PAD : (a + 1) * QUARTER_PAD])
    out[:, FIRST:SECOND] = proj
    out[:, SECOND:] = proto[:, : out.shape[1] - SECOND]


def body(image, section_weights, section_norms, queue, pairing):
    micro, images = image.shape[0], image.shape[2]
    ndp = lax.axis_size("dp")
    t = lax.axis_index("section")
    dp = lax.axis_index("dp")
    place = jnp.stack([t ^ k for k in range(SECTIONS)]).astype(jnp.int32)
    cells = CROPS * PLACES * images
    rows = micro * cells
    count = float(cells * ndp)
    packed = section_weights[0]
    param_rows = packed.shape[0]
    flat = image.transpose(0, 1, 3, 4, 2, 5).reshape(rows, D)

    def part_rows(value):
        size = value.shape[0] // ndp
        return lax.dynamic_slice_in_dim(value, dp * size, size, 0)

    def whole(part):
        return lax.all_gather(part, "dp", axis=0, tiled=True)

    head_rows = part_rows(packed[:D])
    columns = [head_rows[:, j * PART : (j + 1) * PART] for j in range(SECTIONS)]
    got = columns[0]
    came = [send(columns[j], 0, j) for j in range(1, SECTIONS)]
    w_reduce = whole(jnp.where(t == 0, got, came[0] + came[1] + came[2]))

    conv_rows = part_rows(packed[: 9 * WIDTH])
    conv_columns = [conv_rows[:, j * PART : (j + 1) * PART] for j in range(SECTIONS)]
    expand_rows = head_rows.reshape(WIDTH // ndp, 4, WIDTH)
    expand_slices = [expand_rows[:, j] for j in range(SECTIONS)]
    came_c = [send(conv_columns[j], 1, j) for j in (0, 2, 3)]
    w_conv = whole(jnp.where(t == 1, conv_columns[1], came_c[0] + came_c[1] + came_c[2]))
    came_e = [send(expand_slices[j], 2, j) for j in (0, 1, 3)]
    w_expand = whole(jnp.where(t == 2, expand_slices[2], came_e[0] + came_e[1] + came_e[2]))
    by_input = packed[: 9 * WIDTH].reshape(9, SECTIONS, PART, WIDTH)
    back_slices = [part_rows(by_input[:, j].reshape(9 * PART, WIDTH)) for j in range(SECTIONS)]
    came_b = [send(back_slices[j], 1, j) for j in (0, 2, 3)]
    w_conv_back = whole(jnp.where(t == 1, back_slices[1], came_b[0] + came_b[1] + came_b[2]))
    reduce_slices = [part_rows(packed[j * WIDE : (j + 1) * WIDE]) for j in range(SECTIONS)]
    came_r = [send(reduce_slices[j], 0, j) for j in range(1, SECTIONS)]
    w_reduce_back = whole(jnp.where(t == 0, reduce_slices[0], came_r[0] + came_r[1] + came_r[2]))

    norms = lax.all_gather(section_norms[0], "section", axis=0)
    norm0, norm1 = norms[0, :, :WIDTH], norms[1, :, :WIDTH]
    norm2 = lax.dynamic_slice_in_dim(norms[2], t * WIDE, WIDE, 1)
    norm3 = section_norms[0]
    queue_all = lax.all_gather(queue, "dp", axis=1, tiled=True)
    pairing_all = lax.all_gather(pairing.astype(F32), "dp", axis=1, tiled=True).astype(jnp.int32)

    def piece():
        return shape((rows, PART), BF16)

    sums_of = shape((8, PART), F32)
    k = functools.partial

    def exchange(value, sums):
        sums = jnp.stack(gather_xor(sums, "section"))
        pieces = gather_xor(value, "section")
        return pieces, sum_dp(sums.reshape(SECTIONS * 8, PART)).reshape(SECTIONS, 8, PART)

    pre0, part = call(k(reduce_kernel, micro), (piece(), sums_of), flat, w_reduce)
    pre0s, sums0 = exchange(pre0, part)
    active0, pre1, part = call(
        k(conv_kernel, micro, images, count),
        (piece(), piece(), sums_of),
        place, *pre0s, sums0, norm0, w_conv,
        scratch=[pltpu.VMEM((rows, WIDTH), BF16)],
    )
    pre1s, sums1 = exchange(pre1, part)
    active1, pre2, part = call(
        k(expand_kernel, micro, count),
        (shape((rows, WIDTH), BF16), shape((rows, WIDE), F32), shape((8, WIDE), F32)),
        place, *pre1s, sums1, norm1, w_expand,
    )
    sums2 = sum_dp(part)
    pooled = call(
        k(pool_kernel, micro, images, count),
        shape((rows // PLACES, WIDE), BF16),
        place, pre2, sums2, norm2, flat,
    )

    head_order = jnp.arange(rows // PLACES * ndp, dtype=jnp.int32)
    per_dp = rows // PLACES
    block, inner = head_order // per_dp, head_order % per_dp
    group, single = inner // images, inner % images
    position = (group * ndp + (block ^ dp)) * images + single
    order = (position[None, :] == head_order[:, None]).astype(BF16)
    all_pooled = gather_dp(pooled).reshape(per_dp * ndp, WIDE)
    came_p = [send(all_pooled, j, 3) for j in range(3)]
    all_pooled = dot(order, jnp.concatenate(came_p + [all_pooled], axis=1)).astype(BF16)
    w_head = packed[:FIRST].reshape(D, D)
    w_proj = packed[FIRST:SECOND].reshape(D, PROJ)
    table = jnp.pad(packed[SECOND:THIRD], ((0, QUARTER_PAD - QUARTER), (0, 0)))
    protos = jnp.concatenate([table[:, a * PROJ : (a + 1) * PROJ] for a in range(4)], axis=0)
    half = images * ndp
    left = jnp.arange(half, dtype=jnp.int32)
    partner = left // images * images + pairing_all
    match = (partner[:, :, None] == left[None, None, :]).astype(F32)
    loss, grads3, active3, unit, d_scores, d_embed, d_pre3 = head(
        all_pooled, w_head, w_proj, protos, norm3, queue_all, match, micro, images, dp
    )
    d_pooled = dot_nt(dot_tn(order[:, :per_dp], d_pre3).astype(BF16), w_head).astype(BF16)
    parts = [d_pooled[:, j * WIDE : (j + 1) * WIDE] for j in range(SECTIONS)]
    came_d = [send(parts[j], 3, j) for j in range(3)]
    d_pooled = jnp.where(t == 3, parts[3], came_d[0] + came_d[1] + came_d[2])

    d_z, part = call(
        k(out_back_kernel, micro, images, count),
        (shape((rows, WIDE), F32), shape((8, WIDE), F32)),
        place, pre2, sums2, norm2, flat, d_pooled,
    )
    back2 = sum_dp(part)
    d_pre2, *partial = call(
        k(expand_back_kernel, micro, count),
        (shape((rows, WIDE), BF16), piece(), piece(), piece(), piece()),
        place, pre2, sums2, norm2, d_z, back2, w_expand,
        scratch=[pltpu.VMEM((rows, WIDTH), F32)],
    )
    partial = [partial[0]] + [flip(partial[j], "section", j) for j in range(1, SECTIONS)]
    d_y1, part = call(
        k(silu_back_kernel, micro, count),
        (piece(), sums_of),
        place, *partial, pre1, sums1, norm1,
    )
    d_y1s, back1 = exchange(d_y1, part)
    d_pre1, grads1, d_y0, part = call(
        k(conv_back_kernel, micro, images, count),
        (shape((rows, WIDTH), BF16), shape((8, WIDTH), F32), piece(), sums_of),
        place, *d_y1s, back1, *pre1s, sums1, norm1, w_conv_back, pre0, sums0, norm0,
    )
    d_y0s, back0 = exchange(d_y0, part)
    d_pre0, grads0, grad_in = call(
        k(reduce_back_kernel, micro, count),
        (shape((rows, WIDTH), BF16), shape((8, WIDTH), F32), shape((rows, WIDE), F32)),
        place, *d_y0s, back0, *pre0s, sums0, norm0, w_reduce_back, d_z,
    )

    def scatter(value):
        return lax.psum_scatter(value.astype(BF16), "dp", scatter_dimension=0, tiled=True)

    g_expand = scatter(dot_tn(d_pre2, active1))
    taps = call(k(taps_kernel, images), shape((rows, 9 * PART), BF16), active0)
    g_conv = scatter(dot_tn(d_pre1, taps))
    own_image = lax.dynamic_slice_in_dim(flat, t * WIDE, WIDE, 1)
    g_reduce = scatter(dot_tn(d_pre0, own_image))
    own = WIDTH // ndp
    to_conv = [send(g_conv, j, 1) for j in (0, 2, 3)]
    to_expand = [send(g_expand, j, 2) for j in (0, 1, 3)]
    to_reduce = [send(g_reduce, j, 0) for j in (1, 2, 3)]
    pick = (jnp.arange(WIDTH, dtype=jnp.int32)[:, None] == dp * own + jnp.arange(own, dtype=jnp.int32)[None, :]).astype(BF16)
    weave = interleave(PART)

    def fill(value):
        return jnp.pad(value, ((0, 0), (0, param_rows - value.shape[1])))

    def finish_reduce():
        return fill(jnp.concatenate([g_reduce] + to_reduce, axis=1).astype(F32))

    def finish_conv():
        four = [to_conv[0], g_conv, to_conv[1], to_conv[2]]
        cols = [f[:, tap * PART : (tap + 1) * PART] for tap in range(9) for f in four]
        return fill(jnp.concatenate(cols, axis=1).astype(F32))

    def finish_expand():
        four = [to_expand[0], to_expand[1], g_expand, to_expand[2]]
        cols = []
        for b in range(WIDTH // PART):
            mixed = jnp.concatenate([f[:, b * PART : (b + 1) * PART] for f in four], axis=1)
            cols.append(dot(mixed, weave))
        return fill(jnp.concatenate(cols, axis=1))

    def finish_head():
        return call(
            head_grads_kernel,
            shape((own, param_rows), F32),
            all_pooled, active3, unit, d_scores, d_embed, d_pre3, pick, weave,
        )

    weight_grads = lax.switch(t, [finish_reduce, finish_conv, finish_expand, finish_head])
    loss = jnp.where(t == 3, loss, 0.0)
    own_norm = jnp.concatenate([back2[:1] + back2[1:2], back2[micro : micro + 1] + back2[micro + 1 : micro + 2]])
    note = jnp.concatenate([own_norm, jnp.full((1, WIDE), loss), jnp.zeros((5, WIDE), F32)])
    notes = lax.all_gather(note, "section", axis=0)
    loss = jnp.sum(notes[:, 2, 0])
    grads2 = jnp.pad(notes[:, :2].transpose(1, 0, 2).reshape(2, D), ((0, 1), (0, 0)))

    def narrow(value):
        return jnp.pad(value[:3], ((0, 0), (0, D - WIDTH)))

    norm_grads = jnp.where(
        t == 0, narrow(grads0), jnp.where(t == 1, narrow(grads1), jnp.where(t == 2, grads2, grads3))
    )
    grad_in = grad_in.reshape(micro, CROPS, SIDE, SIDE, images, WIDE).transpose(0, 1, 4, 2, 3, 5)
    return (loss, grad_in, weight_grads.T[None], norm_grads[None])


def solution(mesh):
    in_specs = (
        P(None, None, "dp", None, None, None),
        P("section", None, None),
        P("section", None, None),
        P(None, "dp", None),
        P(None, "dp"),
    )
    out_specs = (
        P(),
        P(None, None, "dp", None, None, "section"),
        P("section", None, "dp"),
        P("section", None, None),
    )
    return jax.shard_map(body, mesh=mesh, in_specs=in_specs, out_specs=out_specs, check_vma=False)
```

time: 2360 us -> 567 us (0.24)
  local copies, waits for them, and re-layouts: 923 us -> 143 us
  blocking collectives: 777 us -> 89.1 us
  other arithmetic: 266 us -> 36.6 us
  matrix products: 110 us -> 24.1 us
  starting transfers between devices: 43.4 us -> 122 us
  waiting for transfers between devices: 172 us -> 104 us
  loops' own time: 35.5 us -> 0.04 us
    psum x26 -> x0, blocking collectives: 777 us -> none  [the longest x15 389 us: balance_each(): column = lax.psum(jnp.sum(mass, axis=1), 'dp')]
    unnamed x20 -> x175, local copies, waits for them, and re-layouts: 655 us -> 39.4 us
    all_gather x0 -> x7, blocking collectives: none -> 89.1 us  [the longest x3 47.8 us: whole(): return lax.all_gather(part, 'dp', axis=0, tiled=True)]
    ppermute x10 -> x85, starting transfers between devices: 43.3 us -> 122 us  [the longest x55 68 us: flip(): lax.ppermute(value, axis, [(source, source ^ step) for source in range(co...]
    dot_general x116 -> x15, matrix products: 99.3 us -> 24.1 us  [the longest x3 7.79 us: dot_nt(): return lax.dot_general(a, b, NT, preferred_element_type=F32)]
    scatter-add x5 -> x0, other arithmetic: 61.7 us -> none  [end_conv(): gradient_list.at[:9 * BOTTLENECK_WIDTH]]
    reshape x95 -> x7, local copies, waits for them, and re-layouts: 96.8 us -> 38.9 us  [the longest x2 27.9 us: body(): w_head = packed[:FIRST].reshape(D, D)]
    mul x25 -> x4, other arithmetic: 51.8 us -> 1.23 us  [the longest x1 1.19 us: head(): xhat * by_x / group]
  transfers between devices with their start and end apart: 12 -> 90, of which waited for: 7 -> 29; matrix products, arithmetic and copies ran while one was open for 9% -> 25% of each run, Pallas kernels for 0% -> 4%
where the time goes in v1:
time: 567 us; the launch traced here: 557 us
  local copies, waits for them, and re-layouts  143 us (25%)
  starting transfers between devices  122 us (22%)
  waiting for transfers between devices  104 us (18%)
  blocking collectives  89.1 us (16%)
  other arithmetic  36.6 us (6%)
  matrix products  24.1 us (4%)
  Pallas kernels  22.1 us (4%)
  between operations  16.1 us (3%)
    ppermute x55, starting transfers between devices, flip(): lax.ppermute(value, axis, [(source, source ^ step) for source in range(co...  68 us
    ppermute x55, waiting for transfers between devices, flip(): lax.ppermute(value, axis, [(source, source ^ step) for source in range(co...  55.1 us
    ppermute x30, starting transfers between devices, send(): return lax.ppermute(value, 'section', [(source, target)])  54.3 us
    all_gather x3, blocking collectives, whole(): return lax.all_gather(part, 'dp', axis=0, tiled=True)  47.8 us
    unnamed x175, local copies, waits for them, and re-layouts  39.4 us
    reduce_scatter x3, waiting for transfers between devices, scatter(): lax.psum_scatter(value.astype(BF16), 'dp', scatter_dimension=0, tiled=True)  36.7 us
    reshape x2, local copies, waits for them, and re-layouts, body(): w_head = packed[:FIRST].reshape(D, D)  27.9 us
    cond x35, local copies, waits for them, and re-layouts  25.4 us
  transfers between devices with their start and end apart: 90, of which 29 were waited for; matrix products, arithmetic and copies ran while one was open for 25% of the time, Pallas kernels for 4%

profile of v1, /device:TPU:2, one launch (start us, length us, event | category | flops | bytes accessed | tf_op | source)
XLA Modules:
  0.0 557.0 jit_solution(10056973068566289533)
XLA Ops:
  12.4 4.7 slice.349
  19.2 4.0 collective-permute-start.14
  33.7 12.0 %all-gather.1 = f32[8,4,2]{1,2,0:T(2,128)S(1)} all-gather(f32[1,4,2]{1,2,0:T(2,128)S(1)} %convert_bitcast_fusion), channel_id=1, replica_groups=mesh['section'=4,'dp'=8] {'dp'}, dimensions={0}, use_global_device_ids=true | all-gather | bytes 288 | tf_op jit(solution)/shard_map/all_gather | solution.py:479
  46.6 6.9 %all_gather.31 = f32[4,3,2048]{2,1,0:T(4,128)S(1)} all-gather(f32[1,3,2048]{2,1,0:T(4,128)S(1)} %copy.70), channel_id=1, replica_groups=mesh['section'=4,'dp'=8] {'section'}, dimensions={0}, use_global_device_ids=true | all-gather | bytes 122880 | tf_op jit(solution)/shard_map/all_gather | solution.py:474
  53.6 14.2 %all_gather.35 = bf16[2,512,128]{2,1,0:T(8,128)(2,1)S(1)} all-gather(bf16[2,64,128]{2,1,0:T(8,128)(2,1)S(1)} %copy-done.71), channel_id=1, replica_groups=mesh['section'=4,'dp'=8] {'dp'}, dimensions={1}, use_global_device_ids=true | all-gather | bytes 294912 | tf_op jit(solution)/shard_map/all_gather | solution.py:478
  72.2 4.6 copy-done.43
  83.8 4.6 fusion.137
  89.1 5.1 reshape.541.image
  95.1 17.2 %all_gather.30.weight = bf16[2048,128]{1,0:T(8,128)(2,1)S(1)} all-gather(bf16[256,128]{1,0:T(8,128)(2,1)S(1)} %slice_select_fusion.1), channel_id=1, replica_groups=mesh['section'=4,'dp'=8] {'dp'}, dimensions={0}, use_global_device_ids=true | all-gather | bytes 589824 | tf_op jit(solution)/shard_map/all_gather | solution.py:450
  113.3 4.9 collective-permute-start.8
  132.7 5.3 collective-permute-done.5.p3
  146.9 3.8 shard_map.85
  169.8 14.8 %all_gather.33.weight = bf16[512,512]{1,0:T(8,128)(2,1)S(1)} all-gather(bf16[64,512]{1,0:T(8,128)(2,1)S(1)} %fusion.106), channel_id=1, replica_groups=mesh['section'=4,'dp'=8] {'dp'}, dimensions={0}, use_global_device_ids=true | all-gather | bytes 589824 | tf_op jit(solution)/shard_map/all_gather | solution.py:450
  188.2 5.2 collective-permute-done.18.p3
  211.7 7.3 %slice.362 = bf16[1,8192,512]{2,1,0:T(8,128)(2,1)} slice(bf16[1,9456,512]{2,1,0:T(8,128)(2,1)} %param.10), slice={[0:1], [0:8192], [0:512]} | slice | bytes 16777216 | tf_op jit(solution)/shard_map/slice | solution.py:522
  218.9 14.0 %reshape.564 = bf16[2048,2048,1]{1,0,2:T(8,128)(2,1)} reshape(bf16[1,8192,512]{2,1,0:T(8,128)(2,1)} %slice.362) | data formatting | bytes 16777216 | tf_op jit(solution)/shard_map/reshape | solution.py:522
  232.9 13.9 %reshape.548 = bf16[2048,2048]{1,0:T(8,128)(2,1)} reshape(bf16[1,8192,512]{2,1,0:T(8,128)(2,1)} %slice.362) | data formatting | bytes 16777216 | tf_op jit(solution)/shard_map/reshape | solution.py:522
  273.3 5.0 fusion.131
  306.8 6.0 %convolution_convert_fusion.3 = bf16[16,2048]{1,0:T(8,128)(2,1)S(1)} fusion(bf16[2048,2048]{1,0:T(8,128)(2,1)} %reshape.548, bf16[128,2048]{1,0:T(8,128)(2,1)} %bitcast.293, pred[128,128]{1,0:T(32,128)(4,1)} %iota_compare_fusion.3), kind=kOutput, calls=%fused_computation.119 | convolution fusion | flops 142671872 | bytes 8994816 | tf_op jit(solution)/shard_map/dot_general | solution.py:42
  336.8 5.2 collective-permute-start.47
  343.5 4.5 collective-permute-done.47.q1
  348.0 4.1 collective-permute-done.48.q2
  371.8 3.9 collective-permute-start.51
  388.6 4.7 shard_map.91
  402.0 4.4 collective-permute-done.73
  411.8 15.8 %all_gather.39.weight = bf16[512,512]{1,0:T(8,128)(2,1)S(1)} all-gather(bf16[64,512]{1,0:T(8,128)(2,1)S(1)} %bitcast_select_fusion), channel_id=1, replica_groups=mesh['section'=4,'dp'=8] {'dp'}, dimensions={0}, use_global_device_ids=true | all-gather | bytes 589824 | tf_op jit(solution)/shard_map/all_gather | solution.py:450
  431.1 5.5 collective-permute-done.65.d3
  454.7 8.2 %all-gather = f32[32,512]{1,0:T(8,128)S(1)} all-gather(f32[8,512]{1,0:T(8,128)S(1)} %maximum_maximum_fusion), channel_id=2, replica_groups=mesh['section'=4,'dp'=8] {'section'}, dimensions={0}, use_global_device_ids=true | all-gather | bytes 81920 | tf_op jit(solution)/shard_map/all_gather | solution.py:614
  464.3 4.0 collective-permute-start.83
  469.6 9.3 %reduce-scatter.4.cloned.1.call-done = bf16[64,512]{1,0:T(8,128)(2,1)} async-done(((bf16[512,512]{1,0:T(8,128)(2,1)}), bf16[64,512]{1,0:T(8,128)(2,1)}) %reduce-scatter.4.cloned.1.call-update) | async-done | bytes 65552 | tf_op jit(solution)/shard_map/reduce_scatter | solution.py:570
  485.1 27.4 %reduce-scatter.6.cloned.1.call-done = bf16[64,1152]{1,0:T(8,128)(2,1)} async-done(((bf16[512,1152]{1,0:T(8,128)(2,1)}), bf16[64,1152]{1,0:T(8,128)(2,1)}) %reduce-scatter.6.cloned.1.call-update) | async-done | bytes 147472 | tf_op jit(solution)/shard_map/reduce_scatter | solution.py:570
  522.5 27.8 %conditional.1 = (f32[64,9456]{1,0:T(8,128)}) conditional(s32[]{:T(128)} %clamp.3, (bf16[64,512]{1,0:T(8,128)(2,1)}, bf16[64,512]{1,0:T(8,128)(2,1)}, bf16[64,512]{1,0:T(8,128)(2,1)}, bf16[64,512]{1,0:T(8,128)(2,1)}) %tuple.20, (bf16[64,1152]{1,0:T(8,128)(2,1)}, bf16[64,1152]{1,0:T(8,128)(2,1)}, ...), branch_computations={%region_56.57_spmd, %region_57.58_spmd, %region_58.59_spmd, %regio... | conditional | flops 140107776 | bytes 6352904 | solution.py:610
  (537 shorter events, 290.5 us)
Async XLA Ops:
  7.2 134.7 %all-gather.5.cloned.1.call-start = ((), (), s32[]{:S(2)}) async-start(), calls=%async_computation.3 | async-start | bytes 1327104 | tf_op jit(solution)/shard_map/all_gather | solution.py:450
  9.7 84.4 %collective-permute-start.1 = (bf16[256,128]{1,0:T(8,128)(2,1)}, bf16[256,128]{1,0:T(8,128)(2,1)}, u32[]{:S(2)}, u32[]{:S(2)}) collective-permute-start(bf16[256,128]{1,0:T(8,128)(2,1)} %get-tuple-element.229), channel_id=1, source_target_pairs={{0,16},{1,17},{2,18},{3,19},{4,20},{5,21},{6,22},{7,23}} | collective-permute-start | bytes 196616 | tf_op jit(solution)/shard_map/ppermute | solution.py:55
  11.0 83.1 %collective-permute-start.2 = (bf16[256,128]{1,0:T(8,128)(2,1)}, bf16[256,128]{1,0:T(8,128)(2,1)}, u32[]{:S(2)}, u32[]{:S(2)}) collective-permute-start(bf16[256,128]{1,0:T(8,128)(2,1)} %get-tuple-element.230), channel_id=1, source_target_pairs={{0,24},{1,25},{2,26},{3,27},{4,28},{5,29},{6,30},{7,31}} | collective-permute-start | bytes 196616 | tf_op jit(solution)/shard_map/ppermute | solution.py:55
  19.2 58.8 %collective-permute-start.14 = (bf16[576,128]{1,0:T(8,128)(2,1)}, bf16[576,128]{1,0:T(8,128)(2,1)}, u32[]{:S(2)}, u32[]{:S(2)}) collective-permute-start(bf16[576,128]{1,0:T(8,128)(2,1)} %get-tuple-element.222), channel_id=1, source_target_pairs={{8,16},{9,17},{10,18},{11,19},{12,20},{13,21},{14,22},{15,23}} | collective-permute-start | bytes 442376 | tf_op jit(solution)/shard_map/ppermute | solution.py:55
  23.1 56.2 %collective-permute-start.15 = (bf16[576,128]{1,0:T(8,128)(2,1)}, bf16[576,128]{1,0:T(8,128)(2,1)}, u32[]{:S(2)}, u32[]{:S(2)}) collective-permute-start(bf16[576,128]{1,0:T(8,128)(2,1)} %get-tuple-element.223), channel_id=1, source_target_pairs={{8,24},{9,25},{10,26},{11,27},{12,28},{13,29},{14,30},{15,31}} | collective-permute-start | bytes 442376 | tf_op jit(solution)/shard_map/ppermute | solution.py:55
  25.1 55.5 %collective-permute-start.13 = (bf16[576,128]{1,0:T(8,128)(2,1)}, bf16[576,128]{1,0:T(8,128)(2,1)}, u32[]{:S(2)}, u32[]{:S(2)}) collective-permute-start(bf16[576,128]{1,0:T(8,128)(2,1)} %get-tuple-element.224), channel_id=1, source_target_pairs={{8,0},{9,1},{10,2},{11,3},{12,4},{13,5},{14,6},{15,7}} | collective-permute-start | bytes 442376 | tf_op jit(solution)/shard_map/ppermute | solution.py:55
  79.3 84.4 %collective-permute-start.28 = (bf16[64,512]{1,0:T(8,128)(2,1)}, bf16[64,512]{1,0:T(8,128)(2,1)}, u32[]{:S(2)}, u32[]{:S(2)}) collective-permute-start(bf16[64,512]{1,0:T(8,128)(2,1)} %bitcast.257), channel_id=1, source_target_pairs={{16,24},{17,25},{18,26},{19,27},{20,28},{21,29},{22,30},{23,31}} | collective-permute-start | bytes 196616 | tf_op jit(solution)/shard_map/ppermute | solution.py:55
  80.6 83.1 %collective-permute-start.26 = (bf16[64,512]{1,0:T(8,128)(2,1)}, bf16[64,512]{1,0:T(8,128)(2,1)}, u32[]{:S(2)}, u32[]{:S(2)}) collective-permute-start(bf16[64,512]{1,0:T(8,128)(2,1)} %bitcast.259), channel_id=1, source_target_pairs={{16,0},{17,1},{18,2},{19,3},{20,4},{21,5},{22,6},{23,7}} | collective-permute-start | bytes 196616 | tf_op jit(solution)/shard_map/ppermute | solution.py:55
  83.7 292.0 %all-gather.7.cloned.1.call-start = ((), (), s32[]{:S(2)}) async-start(), calls=%async_computation.4 | async-start | bytes 1327104 | tf_op jit(solution)/shard_map/all_gather | solution.py:450
  158.7 110.0 %collective-permute-start.62 = (bf16[144,512]{1,0:T(8,128)(2,1)}, bf16[144,512]{1,0:T(8,128)(2,1)}, u32[]{:S(2)}, u32[]{:S(2)}) collective-permute-start(bf16[144,512]{1,0:T(8,128)(2,1)} %constant_dynamic-slice_fusion), channel_id=1, source_target_pairs={{8,24},{9,25},{10,26},{11,27},{12,28},{13,29},{14,30},{15,31}} | collective-permute-start | bytes 442376 | tf_op jit(solution)/shard_map/ppermute | solution.py:55
  161.7 108.3 %collective-permute-start.60 = (bf16[144,512]{1,0:T(8,128)(2,1)}, bf16[144,512]{1,0:T(8,128)(2,1)}, u32[]{:S(2)}, u32[]{:S(2)}) collective-permute-start(bf16[144,512]{1,0:T(8,128)(2,1)} %constant_dynamic-slice_fusion.2), channel_id=1, source_target_pairs={{8,0},{9,1},{10,2},{11,3},{12,4},{13,5},{14,6},{15,7}} | collective-permute-start | bytes 442376 | tf_op jit(solution)/shard_map/ppermute | solution.py:55
  165.4 19.3 %collective-permute-start.25 = (f32[32,128]{1,0:T(8,128)S(1)}, f32[32,128]{1,0:T(8,128)S(1)}, u32[]{:S(2)}, u32[]{:S(2)}) collective-permute-start(f32[32,128]{1,0:T(8,128)S(1)} %fusion.127), channel_id=1, source_target_pairs={{0,6},{1,7},{2,4},{3,5},{4,2},{5,3},{6,0},{7,1},{8,14},{9,15},{10,... | collective-permute-start | bytes 49160 | tf_op jit(solution)/shard_map/ppermute | solution.py:51
  166.1 19.3 %collective-permute-start.24 = (f32[32,128]{1,0:T(8,128)S(1)}, f32[32,128]{1,0:T(8,128)S(1)}, u32[]{:S(2)}, u32[]{:S(2)}) collective-permute-start(f32[32,128]{1,0:T(8,128)S(1)} %fusion.127), channel_id=1, source_target_pairs={{0,4},{1,5},{2,6},{3,7},{4,0},{5,1},{6,2},{7,3},{8,12},{9,13},{10,... | collective-permute-start | bytes 49160 | tf_op jit(solution)/shard_map/ppermute | solution.py:51
  166.7 18.7 %collective-permute-start.23 = (f32[32,128]{1,0:T(8,128)S(1)}, f32[32,128]{1,0:T(8,128)S(1)}, u32[]{:S(2)}, u32[]{:S(2)}) collective-permute-start(f32[32,128]{1,0:T(8,128)S(1)} %fusion.127), channel_id=1, source_target_pairs={{0,2},{1,3},{2,0},{3,1},{4,6},{5,7},{6,4},{7,5},{8,10},{9,11},{10,... | collective-permute-start | bytes 49160 | tf_op jit(solution)/shard_map/ppermute | solution.py:51
  202.9 43.9 %collective-permute-start.32 = (f32[8,512]{1,0:T(8,128)S(1)}, f32[8,512]{1,0:T(8,128)S(1)}, u32[]{:S(2)}, u32[]{:S(2)}) collective-permute-start(f32[8,512]{1,0:T(8,128)S(1)} %add.421), channel_id=1, source_target_pairs={{0,6},{1,7},{2,4},{3,5},{4,2},{5,3},{6,0},{7,1},{8,14},{9,15},{10,... | collective-permute-start | bytes 49160 | tf_op jit(solution)/shard_map/ppermute | solution.py:51
  203.4 46.6 %collective-permute-start.31 = (f32[8,512]{1,0:T(8,128)S(1)}, f32[8,512]{1,0:T(8,128)}, u32[]{:S(2)}, u32[]{:S(2)}) collective-permute-start(f32[8,512]{1,0:T(8,128)S(1)} %add.421), channel_id=1, source_target_pairs={{0,4},{1,5},{2,6},{3,7},{4,0},{5,1},{6,2},{7,3},{8,12},{9,13},{10,... | collective-permute-start | bytes 49160 | tf_op jit(solution)/shard_map/ppermute | solution.py:51
  203.6 46.3 %collective-permute-start.30 = (f32[8,512]{1,0:T(8,128)S(1)}, f32[8,512]{1,0:T(8,128)}, u32[]{:S(2)}, u32[]{:S(2)}) collective-permute-start(f32[8,512]{1,0:T(8,128)S(1)} %add.421), channel_id=1, source_target_pairs={{0,2},{1,3},{2,0},{3,1},{4,6},{5,7},{6,4},{7,5},{8,10},{9,11},{10,... | collective-permute-start | bytes 49160 | tf_op jit(solution)/shard_map/ppermute | solution.py:51
  246.8 23.2 %collective-permute-start.61 = (bf16[144,512]{1,0:T(8,128)(2,1)}, bf16[144,512]{1,0:T(8,128)(2,1)S(1)}, u32[]{:S(2)}, u32[]{:S(2)}) collective-permute-start(bf16[144,512]{1,0:T(8,128)(2,1)} %constant_dynamic-slice_fusion.1), channel_id=1, source_target_pairs={{8,16},{9,17},{10,18},{11,19},{12,20},{13,21},{14,22},{15,23}} | collective-permute-start | bytes 442376 | tf_op jit(solution)/shard_map/ppermute | solution.py:55
  271.8 191.2 %reduce-scatter.8.cloned.1.call-start = ((), (), s32[]{:S(2)}) async-start(), calls=%async_computation.7 | async-start | bytes 589824 | tf_op jit(solution)/shard_map/reduce_scatter | solution.py:570
  360.1 41.9 %collective-permute-start.74 = (bf16[64,512]{1,0:T(8,128)(2,1)}, bf16[64,512]{1,0:T(8,128)(2,1)}, u32[]{:S(2)}, u32[]{:S(2)}) collective-permute-start(bf16[64,512]{1,0:T(8,128)(2,1)} %dynamic-slice_bitcast_fusion.2), channel_id=1, source_target_pairs={{0,16},{1,17},{2,18},{3,19},{4,20},{5,21},{6,22},{7,23}} | collective-permute-start | bytes 196616 | tf_op jit(solution)/shard_map/ppermute | solution.py:55
  362.9 39.1 %collective-permute-start.75 = (bf16[64,512]{1,0:T(8,128)(2,1)}, bf16[64,512]{1,0:T(8,128)(2,1)}, u32[]{:S(2)}, u32[]{:S(2)}) collective-permute-start(bf16[64,512]{1,0:T(8,128)(2,1)} %dynamic-slice_bitcast_fusion.1), channel_id=1, source_target_pairs={{0,24},{1,25},{2,26},{3,27},{4,28},{5,29},{6,30},{7,31}} | collective-permute-start | bytes 196616 | tf_op jit(solution)/shard_map/ppermute | solution.py:55
  400.0 78.9 %reduce-scatter.4.cloned.1.call-start = ((), (), s32[]{:S(2)}) async-start(), calls=%async_computation.5 | async-start | bytes 589824 | tf_op jit(solution)/shard_map/reduce_scatter | solution.py:570
  407.4 21.4 %collective-permute-start.72 = (f32[32,128]{1,0:T(8,128)S(1)}, f32[32,128]{1,0:T(8,128)S(1)}, u32[]{:S(2)}, u32[]{:S(2)}) collective-permute-start(f32[32,128]{1,0:T(8,128)S(1)} %fusion.125), channel_id=1, source_target_pairs={{0,6},{1,7},{2,4},{3,5},{4,2},{5,3},{6,0},{7,1},{8,14},{9,15},{10,... | collective-permute-start | bytes 49160 | tf_op jit(solution)/shard_map/ppermute | solution.py:51
  409.3 21.8 %collective-permute-start.71 = (f32[32,128]{1,0:T(8,128)S(1)}, f32[32,128]{1,0:T(8,128)S(1)}, u32[]{:S(2)}, u32[]{:S(2)}) collective-permute-start(f32[32,128]{1,0:T(8,128)S(1)} %fusion.125), channel_id=1, source_target_pairs={{0,4},{1,5},{2,6},{3,7},{4,0},{5,1},{6,2},{7,3},{8,12},{9,13},{10,... | collective-permute-start | bytes 49160 | tf_op jit(solution)/shard_map/ppermute | solution.py:51
  409.3 21.8 %collective-permute-start.70 = (f32[32,128]{1,0:T(8,128)S(1)}, f32[32,128]{1,0:T(8,128)S(1)}, u32[]{:S(2)}, u32[]{:S(2)}) collective-permute-start(f32[32,128]{1,0:T(8,128)S(1)} %fusion.125), channel_id=1, source_target_pairs={{0,2},{1,3},{2,0},{3,1},{4,6},{5,7},{6,4},{7,5},{8,10},{9,11},{10,... | collective-permute-start | bytes 49160 | tf_op jit(solution)/shard_map/ppermute | solution.py:51
  449.1 63.4 %reduce-scatter.6.cloned.1.call-start = ((), (), s32[]{:S(2)}) async-start(), calls=%async_computation.6 | async-start | bytes 1327104 | tf_op jit(solution)/shard_map/reduce_scatter | solution.py:570
  463.0 19.1 %collective-permute-start.84 = (bf16[64,512]{1,0:T(8,128)(2,1)}, bf16[64,512]{1,0:T(8,128)(2,1)}, u32[]{:S(2)}, u32[]{:S(2)}) collective-permute-start(bf16[64,512]{1,0:T(8,128)(2,1)} %reduce-scatter.8.cloned.1.call-done), channel_id=1, source_target_pairs={{24,16},{25,17},{26,18},{27,19},{28,20},{29,21},{30,22},{31,23}} | collective-permute-start | bytes 196616 | tf_op jit(solution)/shard_map/ppermute | solution.py:55
  464.3 20.9 %collective-permute-start.83 = (bf16[64,512]{1,0:T(8,128)(2,1)}, bf16[64,512]{1,0:T(8,128)(2,1)}, u32[]{:S(2)}, u32[]{:S(2)}) collective-permute-start(bf16[64,512]{1,0:T(8,128)(2,1)} %reduce-scatter.8.cloned.1.call-done), channel_id=1, source_target_pairs={{8,16},{9,17},{10,18},{11,19},{12,20},{13,21},{14,22},{15,23}} | collective-permute-start | bytes 196616 | tf_op jit(solution)/shard_map/ppermute | solution.py:55
  468.3 45.5 %collective-permute-start.82 = (bf16[64,512]{1,0:T(8,128)(2,1)}, bf16[64,512]{1,0:T(8,128)(2,1)}, u32[]{:S(2)}, u32[]{:S(2)}) collective-permute-start(bf16[64,512]{1,0:T(8,128)(2,1)} %reduce-scatter.8.cloned.1.call-done), channel_id=1, source_target_pairs={{0,16},{1,17},{2,18},{3,19},{4,20},{5,21},{6,22},{7,23}} | collective-permute-start | bytes 196616 | tf_op jit(solution)/shard_map/ppermute | solution.py:55
  478.9 36.2 %collective-permute-start.78 = (bf16[64,512]{1,0:T(8,128)(2,1)}, bf16[64,512]{1,0:T(8,128)(2,1)}, u32[]{:S(2)}, u32[]{:S(2)}) collective-permute-start(bf16[64,512]{1,0:T(8,128)(2,1)} %reduce-scatter.4.cloned.1.call-done), channel_id=1, source_target_pairs={{24,0},{25,1},{26,2},{27,3},{28,4},{29,5},{30,6},{31,7}} | collective-permute-start | bytes 196616 | tf_op jit(solution)/shard_map/ppermute | solution.py:55
  480.8 38.2 %collective-permute-start.77 = (bf16[64,512]{1,0:T(8,128)(2,1)}, bf16[64,512]{1,0:T(8,128)(2,1)}, u32[]{:S(2)}, u32[]{:S(2)}) collective-permute-start(bf16[64,512]{1,0:T(8,128)(2,1)} %reduce-scatter.4.cloned.1.call-done), channel_id=1, source_target_pairs={{16,0},{17,1},{18,2},{19,3},{20,4},{21,5},{22,6},{23,7}} | collective-permute-start | bytes 196616 | tf_op jit(solution)/shard_map/ppermute | solution.py:55
  482.0 36.9 %collective-permute-start.76 = (bf16[64,512]{1,0:T(8,128)(2,1)}, bf16[64,512]{1,0:T(8,128)(2,1)}, u32[]{:S(2)}, u32[]{:S(2)}) collective-permute-start(bf16[64,512]{1,0:T(8,128)(2,1)} %reduce-scatter.4.cloned.1.call-done), channel_id=1, source_target_pairs={{8,0},{9,1},{10,2},{11,3},{12,4},{13,5},{14,6},{15,7}} | collective-permute-start | bytes 196616 | tf_op jit(solution)/shard_map/ppermute | solution.py:55
  (142 other events, 1305.9 us)
Sparse Core Ops, SparseCore 0:
  83.8 26.6 all-gather.4
  271.9 22.8 all-gather.6
  400.1 30.6 reduce-scatter.7
  449.3 29.5 reduce-scatter.3
  481.6 30.8 reduce-scatter.5
